TPU v7x, 256 devices: a whole 4x4x8 slice. The times are simulated.
256 devices in a mesh: px: 16 (over x, z_hi, core), py: 16 (over y, z_lo).
Axes of the slice: x: 4, y: 4, z: 8 (z_hi: 2, z_lo: 4; z = z_hi * 4 + z_lo), core: 2. Of those that a mesh axis runs over, the one named last changes fastest.
Arguments:
- fluid: float32 [3, 512, 32, 2048], P(None, 'px', 'py'), may hold values from -6 to 6
- part_vel: float32 [3, 64, 64, 1024], P(None, 'px', 'py'), may hold values from -6 to 6
- part_frac: float32 [3, 64, 64, 1024], P(None, 'px', 'py'), may hold values from -0.5 to 0.5
- stokes_time: float32 [64, 64, 1024], P('px', 'py'), may hold values from 0.5 to 5
- cells: int32 [64, 64, 1024], P('px', 'py'), may hold values from 0 to 8191
- counts: int32 [64, 64], P('px', 'py'), may hold values from 96 to 1024, as said below
Outputs:
- fluid_next: float32 [3, 512, 32, 2048], P(None, 'px', 'py')
- vel_next: float32 [3, 64, 64, 1024], P(None, 'px', 'py')
Inputs may be any that keep to these rules, and one draw needn't show every extreme that they name: cells = (ix * 32 + iy) * 32 + iz with ix, iy, iz the particle's cell in its sub-brick of 8 x 32 x 32 cells. Slots 0 to counts - 1 of a sub-brick hold live particles, the others are padding; some sub-brick is full.
All inputs are finite; a program needn't handle non-finite values.
Results may differ from a plain program's by a relative error of at most 0.0011.
Values may be sent and summed in bfloat16 or wider, within the bound.
No kernel may reach another device: no remote copies, remote signals or barrier semaphores. Data moves between devices by JAX's collectives and lax.ppermute only.
A program may use at most 64 MiB of HBM per device.

v0:
```python
import functools
import math

import jax
import jax.numpy as jnp
import numpy as np
from jax import lax
from jax.experimental import pallas as pl
from jax.experimental.pallas import tpu as pltpu
from jax.sharding import PartitionSpec as P

mass_load = 4.0
step_dt = 0.5
viscous_step = 0.25
forcing_gain = 1.5
forced_modes = 4

COMPS = 3
LANES = 128
VMEM_LIMIT = 32 * 1024 * 1024
f32 = jnp.float32
bf16 = jnp.bfloat16
NT = (((1,), (1,)), ((), ()))


def filter_blocks(length, width):
    k = np.fft.fftfreq(length, 1.0 / length)
    angle = 2.0 * math.pi * k / length
    gain = np.exp(-viscous_step * angle * angle)
    gain = gain * np.where((abs(k) >= 1) & (abs(k) <= forced_modes), 1.0 + forcing_gain, 1.0)
    taps = np.fft.ifft(gain).real
    blocks = length // width
    half = blocks // 2
    inner = np.arange(width)
    full = []
    for d in range(blocks):
        full.append(taps[(width * d + inner[None, :] - inner[:, None]) % length])
    sums = np.stack([0.5 * (full[d] + full[d + half]) for d in range(half)])
    diffs = np.stack([0.5 * (full[d] - full[d + half]) for d in range(half)])
    both = np.stack([sums, diffs]).astype(np.float32)
    high = both.astype(jnp.bfloat16)
    low = (both - high.astype(np.float32)).astype(jnp.bfloat16)
    return high, low


def pack_kernel(dims, grid_ref, before_ref, after_ref, out_ref, msg):
    width, devices, planes = dims
    span = width + 2
    rows = COMPS * span
    used = planes * rows
    total = out_ref.shape[1]
    for j in range(devices):
        base = j * total
        msg[pl.ds(base + used, total - used), :] = jnp.zeros((total - used, LANES), f32)
        for p in range(planes):
            for c in range(COMPS):
                at = base + p * rows + c * span
                e = p * COMPS + c
                lanes = slice(j * LANES, (j + 1) * LANES)
                msg[pl.ds(at, 1), :] = before_ref[e : e + 1, lanes].astype(f32)
                msg[pl.ds(at + 1, width), :] = grid_ref[
                    pl.ds(c * width * devices * planes + j * planes + p, width, stride=devices * planes), :
                ]
                msg[pl.ds(at + 1 + width, 1), :] = after_ref[e : e + 1, lanes].astype(f32)
    row_id = lax.broadcasted_iota(jnp.int32, (8, LANES), 0)
    lane_id = lax.broadcasted_iota(jnp.int32, (8, LANES), 1)
    pick = ((row_id == 0) & (lane_id == LANES - 1)) | ((row_id == 1) & (lane_id == 0))
    pick = jnp.where(pick, 1.0, 0.0).astype(bf16)
    for j in range(devices):
        for p in range(planes):
            block = msg[pl.ds(j * total + p * rows, rows), :].astype(bf16)
            edge = lax.dot_general(pick, block, NT, preferred_element_type=f32)
            right = (j + 1) % devices
            left = (j - 1) % devices
            msg[pl.ds(right * total + used + 2 * p, 1), 0:rows] = edge[0:1]
            msg[pl.ds(left * total + used + 2 * p + 1, 1), 0:rows] = edge[1:2]
    for j in range(devices):
        out_ref[j] = msg[pl.ds(j * total, total), :].astype(bf16)


def same_cell(c, span, depth, rows):
    row = lax.broadcasted_iota(jnp.int32, (rows, LANES), 0)
    col = lax.broadcasted_iota(jnp.int32, (rows, LANES), 1)
    return jnp.where(row // depth == col - c * span, 1.0, 0.0).astype(bf16)


def side_lane(depth, shape, dim):
    ghost = lax.broadcasted_iota(jnp.int32, shape, dim)
    lane = lax.broadcasted_iota(jnp.int32, shape, 1 - dim)
    hit = ((ghost < depth) & (lane == LANES - 1)) | ((ghost >= depth) & (lane == 0))
    return jnp.where(hit, 1.0, 0.0).astype(bf16)


def particle_kernel(
    dims, counts_ref, recv_ref, vel_ref, frac_ref, tau_ref, cells_ref,
    vel_out_ref, send_ref, msg, rows_buf, ghost, field, deposit, prep, ints,
):
    width, devices, planes, subs_x, subs_y, slots, chunk = dims
    span = width + 2
    depth = devices * planes
    tile_x = width // subs_x
    tile_y = LANES // subs_y
    total = recv_ref.shape[1]
    rows = COMPS * span
    used = planes * rows
    cells = span * depth
    near = 4
    pair = 2 * depth
    pairs = tile_x // 2
    core = cells - pair
    block = near * depth

    for s in range(devices):
        msg[...] = recv_ref[s].astype(f32)
        for p in range(planes):
            z = s * planes + p
            for c in range(COMPS):
                rows_buf[pl.ds(c * cells + z, span, stride=depth), :] = msg[
                    pl.ds(p * rows + c * span, span), :
                ]
            ghost[pl.ds(z, 1), :] = msg[pl.ds(used + 2 * p, 1), :]
            ghost[pl.ds(depth + z, 1), :] = msg[pl.ds(used + 2 * p + 1, 1), :]
    own_z = lax.broadcasted_iota(jnp.int32, (cells, 2 * depth), 0) % depth
    own_z = own_z == lax.broadcasted_iota(jnp.int32, (cells, 2 * depth), 1) % depth
    lane = lax.broadcasted_iota(jnp.int32, (cells, LANES), 1)
    for c in range(COMPS):
        at = pl.ds(c * cells, cells)
        wide = lax.dot_general(
            same_cell(c, span, depth, cells), ghost[...].astype(bf16), NT, preferred_element_type=f32
        )
        wide = jnp.where(own_z, wide, 0.0).astype(bf16)
        outer = jnp.dot(wide, side_lane(depth, (2 * depth, LANES), 0), preferred_element_type=f32)
        inner = rows_buf[at, :]
        lower = jnp.where(lane == LANES - 1, outer, inner)
        upper = jnp.where(lane == 0, outer, inner)
        core = cells - pair
        lane_id = lane[:core]
        for b in range(subs_y):
            value = lower if 2 * b < subs_y else upper
            moved = jnp.roll(value[pair:], LANES // 2, axis=1)
            first_half = (lane_id - (b * tile_y - 16)) % LANES < LANES // 2
            field[b, pl.ds(c * core, core), :] = jnp.where(first_half, value[:core], moved).astype(bf16)

    x_rows = lax.broadcasted_iota(jnp.int32, (8, chunk), 0)
    z_rows = lax.broadcasted_iota(jnp.int32, (depth, chunk), 0)
    y_rows = lax.broadcasted_iota(jnp.int32, (tile_y + 16, chunk), 0) - 8

    def strip(a, carry):
        for d in range(COMPS):
            f = frac_ref[d, a]
            prep[3 * d] = 0.5 * (0.5 - f) ** 2
            prep[3 * d + 1] = 0.75 - f * f
            prep[3 * d + 2] = 0.5 * (0.5 + f) ** 2
        prep[9] = step_dt / tau_ref[a]
        cell = cells_ref[a]
        ints[0] = cell // (tile_y * depth)
        ints[1] = cell // depth % tile_y
        ints[2] = cell % depth
        first = a * (tile_x * depth)

        for b in range(subs_y):
            filled = counts_ref[a, b]
            blocks = tile_x * depth // block
            data = jnp.concatenate(
                [
                    jnp.concatenate(
                        [
                            field[b, pl.ds(pl.multiple_of(c * core + first + t * block, block), block), :]
                            for t in range(blocks)
                        ],
                        axis=1,
                    )
                    for c in range(COMPS)
                ],
                axis=0,
            )
            acc = None
            for start in range(0, slots, chunk):
                at = slice(start, start + chunk)
                row = lambda i: prep[i, b : b + 1, at]
                xc, yc, zc = (ints[i, b : b + 1, at] for i in range(3))
                here = lax.broadcasted_iota(jnp.int32, (1, chunk), 1) + start < filled
                dx = x_rows - (xc & 1)
                wx = jnp.where(
                    dx == 0, row(0), jnp.where(dx == 1, row(1), jnp.where(dx == 2, row(2), 0.0))
                )
                dy = y_rows - yc
                y_low, y_mid, y_high = (jnp.where(here, row(3 + i), 0.0) for i in range(3))
                wy = jnp.where(
                    dy == -1, y_low, jnp.where(dy == 0, y_mid, jnp.where(dy == 1, y_high, 0.0))
                )
                dz = (z_rows - zc + 1) & (depth - 1)
                wz = jnp.where(
                    dz == 0, row(6), jnp.where(dz == 1, row(7), jnp.where(dz == 2, row(8), 0.0))
                )
                groups = LANES // 8
                half_groups = groups // 2
                blank = jnp.zeros((8, chunk), f32)
                pieces = [blank] * (groups * blocks)
                for k in range(pairs):
                    chosen = xc >> 1 == k
                    for g in range(tile_y // 8 + 2):
                        place = (b * tile_y // 8 - 1 + g + (k % 2) * half_groups) % groups
                        pieces[k // 2 * groups + place] = jnp.where(chosen, wy[8 * g : 8 * g + 8], 0.0)
                wy = jnp.concatenate(pieces, axis=0).astype(bf16)
                raw = jnp.dot(data, wy, preferred_element_type=f32)
                rate = row(9)
                shares = []
                for c in range(COMPS):
                    found = None
                    for i in range(near):
                        part = None
                        for g in range(depth // 8):
                            at8 = c * block + i * depth + 8 * g
                            term = raw[at8 : at8 + 8] * wz[8 * g : 8 * g + 8]
                            part = term if part is None else part + term
                        part = part * wx[i : i + 1]
                        found = part if found is None else found + part
                    interp = jnp.sum(found, axis=0, keepdims=True)
                    velocity = vel_ref[c, a, b : b + 1, at]
                    change = rate * (interp - velocity)
                    vel_out_ref[c, a, b : b + 1, at] = jnp.where(here, velocity + change, velocity)
                    pull = jnp.where(here, -mass_load * change, 0.0) * wx
                    shares = shares + [(pull[i : i + 1] * wz).astype(bf16) for i in range(near)]
                part = lax.dot_general(
                    jnp.concatenate(shares, axis=0), wy, NT, preferred_element_type=f32
                )
                acc = part if acc is None else acc + part
            for c in range(COMPS):
                for t in range(blocks):
                    base = pl.multiple_of(c * core + first + t * block, block)
                    deposit[b, pl.ds(base, block), :] = acc[
                        c * block : (c + 1) * block, t * LANES : (t + 1) * LANES
                    ]
        return carry

    lax.fori_loop(0, subs_x, strip, 0)

    gathered = jnp.zeros((2 * depth, LANES), f32)
    for c in range(COMPS):
        at = pl.ds(c * cells, cells)
        sides = []
        lane_id = lane[:core]
        empty = jnp.zeros((pair, LANES), f32)
        for side in range(2):
            even = odd = None
            for b in range(side * subs_y // 2, (side + 1) * subs_y // 2):
                value = deposit[b, pl.ds(c * core, core), :]
                first_half = (lane_id - (b * tile_y - 16)) % LANES < LANES // 2
                one = jnp.where(first_half, value, 0.0)
                two = jnp.where(first_half, 0.0, value)
                even = one if even is None else even + one
                odd = two if odd is None else odd + two
            moved = jnp.roll(odd, LANES // 2, axis=1)
            sides.append(
                jnp.concatenate([even, empty], axis=0) + jnp.concatenate([empty, moved], axis=0)
            )
        lower, upper = sides
        first_lane = lane == 0
        last_lane = lane == LANES - 1
        rows_buf[at, :] = jnp.where(last_lane, 0.0, lower) + jnp.where(first_lane, 0.0, upper)
        outer = jnp.where(last_lane, lower, jnp.where(first_lane, upper, 0.0)).astype(bf16)
        wide = jnp.dot(outer, side_lane(depth, (LANES, 2 * depth), 1), preferred_element_type=f32)
        wide = jnp.where(own_z, wide, 0.0).astype(bf16)
        gathered = gathered + lax.dot_general(
            wide, same_cell(c, span, depth, cells), (((0,), (0,)), ((), ())), preferred_element_type=f32
        )
    ghost[...] = gathered
    for s in range(devices):
        for p in range(planes):
            z = s * planes + p
            for c in range(COMPS):
                msg[pl.ds(p * rows + c * span, span), :] = rows_buf[
                    pl.ds(c * cells + z, span, stride=depth), :
                ]
            msg[pl.ds(used + 2 * p, 1), :] = ghost[pl.ds(z, 1), :]
            msg[pl.ds(used + 2 * p + 1, 1), :] = ghost[pl.ds(depth + z, 1), :]
        send_ref[s] = msg[...].astype(bf16)


def particle_call(dims, counts, recv, part_vel, part_frac, stokes_time, cells):
    width, devices, planes, subs_x, subs_y, slots, chunk = dims
    vmem = pl.BlockSpec(memory_space=pltpu.VMEM)
    total = recv.shape[1]
    depth = devices * planes
    all_rows = COMPS * (width + 2) * depth
    core_rows = COMPS * width * depth
    return pl.pallas_call(
        functools.partial(particle_kernel, dims),
        out_shape=(jax.ShapeDtypeStruct(part_vel.shape, f32), jax.ShapeDtypeStruct(recv.shape, bf16)),
        in_specs=[pl.BlockSpec(memory_space=pltpu.SMEM)] + [vmem] * 5,
        out_specs=(vmem, vmem),
        scratch_shapes=[
            pltpu.VMEM((total, LANES), f32),
            pltpu.VMEM((all_rows, LANES), f32),
            pltpu.VMEM((2 * depth, LANES), f32),
            pltpu.VMEM((subs_y, core_rows, LANES), bf16),
            pltpu.VMEM((subs_y, core_rows, LANES), f32),
            pltpu.VMEM((10, subs_y, slots), f32),
            pltpu.VMEM((3, subs_y, slots), jnp.int32),
        ],
        compiler_params=pltpu.CompilerParams(vmem_limit_bytes=VMEM_LIMIT),
        name="particles",
    )(counts, recv, part_vel, part_frac, stokes_time, cells)


def gather_kernel(dims, recv_ref, out_ref, low_ref, high_ref, msg):
    width, devices, planes = dims
    span = width + 2
    rows = COMPS * span
    used = planes * rows
    total = recv_ref.shape[1]
    count = devices
    for j in range(count):
        msg[j] = recv_ref[j].astype(f32)
    side = lax.broadcasted_iota(jnp.int32, (8, LANES), 0)
    lane = lax.broadcasted_iota(jnp.int32, (8, LANES), 1)
    place = ((side == 0) & (lane == LANES - 1)) | ((side == 1) & (lane == 0))
    place = jnp.where(place, 1.0, 0.0).astype(bf16)
    for j in range(count):
        left = (j - 1) % count
        right = (j + 1) % count
        lanes = slice(j * LANES, (j + 1) * LANES)
        lows, highs = [], []
        for p in range(planes):
            pair = jnp.concatenate(
                [
                    msg[right, used + 2 * p : used + 2 * p + 1, :],
                    msg[left, used + 2 * p + 1 : used + 2 * p + 2, :],
                    jnp.zeros((6, LANES), f32),
                ],
                axis=0,
            ).astype(bf16)
            added = lax.dot_general(
                pair, place, (((0,), (0,)), ((), ())), preferred_element_type=f32
            )
            block = msg[j, p * rows : (p + 1) * rows, :] + added[:rows]
            for c in range(COMPS):
                e = p * COMPS + c
                at = c * span
                lows.append(block[at : at + 1])
                highs.append(block[at + span - 1 : at + span])
                out_ref[pl.ds(e * width, width), lanes] = block[at + 1 : at + 1 + width]
        low_ref[:, lanes] = jnp.concatenate(lows, axis=0).astype(bf16)
        high_ref[:, lanes] = jnp.concatenate(highs, axis=0).astype(bf16)


def filter_kernel(dims, grid_ref, dep_ref, from_low_ref, from_high_ref, high_ref, low_ref, out_ref, mixed):
    width, devices, planes = dims
    depth = devices * planes
    for j in range(devices):
        lanes = slice(j * LANES, (j + 1) * LANES)
        for p in range(planes):
            for c in range(COMPS):
                e = p * COMPS + c
                dep = dep_ref[pl.ds(e * width, width), lanes]
                first = dep[:1] + from_low_ref[e : e + 1, lanes].astype(f32)
                last = dep[width - 1 :] + from_high_ref[e : e + 1, lanes].astype(f32)
                dep = jnp.concatenate([first, dep[1 : width - 1], last], axis=0)
                fluid = grid_ref[pl.ds(c * width * depth + j * planes + p, width, stride=depth), :]
                mixed[pl.ds(e * width, width), lanes] = fluid + dep.astype(bf16).astype(f32)
    folds = high_ref.shape[1]
    block = high_ref.shape[2]
    sides = []
    for sign in range(2):
        highs, lows = [], []
        for i in range(folds):
            one = mixed[:, i * block : (i + 1) * block]
            two = mixed[:, (i + folds) * block : (i + folds + 1) * block]
            value = one + two if sign == 0 else one - two
            high = value.astype(bf16)
            highs.append(high)
            lows.append((value - high.astype(f32)).astype(bf16))
        sides.append((highs, lows))
    for o in range(folds):
        results = []
        for sign in range(2):
            highs, lows = sides[sign]
            sums = {1: None, -1: None}
            for i in range(folds):
                d = (o - i) % folds
                key = -1 if sign == 1 and o < i else 1
                part = jnp.dot(highs[i], high_ref[sign, d], preferred_element_type=f32)
                part = part + jnp.dot(lows[i], high_ref[sign, d], preferred_element_type=f32)
                part = part + jnp.dot(highs[i], low_ref[sign, d], preferred_element_type=f32)
                sums[key] = part if sums[key] is None else sums[key] + part
            results.append(sums[1] if sums[-1] is None else sums[1] - sums[-1])
        for flip in range(2):
            value = results[0] + results[1] if flip == 0 else results[0] - results[1]
            for half in range(block // LANES):
                j = (o + flip * folds) * (block // LANES) + half
                for p in range(planes):
                    for c in range(COMPS):
                        e = p * COMPS + c
                        out_ref[pl.ds(c * width * depth + j * planes + p, width, stride=depth), :] = value[
                            e * width : (e + 1) * width, half * LANES : (half + 1) * LANES
                        ]


def per_device(fluid, part_vel, part_frac, stokes_time, cells, counts):
    devices = lax.axis_size("py")
    rows_px = lax.axis_size("px")
    _, width, planes, length = fluid.shape
    subs_x, subs_y, slots = stokes_time.shape
    depth = planes * devices
    span = width + 2
    used = planes * COMPS * span
    total = -(-(used + 2 * planes) // 16) * 16
    up = [(i, (i + 1) % rows_px) for i in range(rows_px)]
    down = [(j, i) for i, j in up]
    params = pltpu.CompilerParams(vmem_limit_bytes=VMEM_LIMIT)
    vmem = pl.BlockSpec(memory_space=pltpu.VMEM)

    edges = jnp.stack([fluid[:, 0], fluid[:, width - 1]])
    edges = edges.transpose(0, 2, 1, 3).reshape(2, planes * COMPS, length).astype(bf16)
    before = lax.ppermute(edges[1], "px", up)
    after = lax.ppermute(edges[0], "px", down)
    grid = fluid.reshape(COMPS * width, planes, devices, LANES).transpose(0, 2, 1, 3)
    grid = grid.reshape(COMPS * width * depth, LANES)
    dims = (width, devices, planes)
    send = pl.pallas_call(
        functools.partial(pack_kernel, dims),
        out_shape=jax.ShapeDtypeStruct((devices, total, LANES), bf16),
        in_specs=[vmem] * 3,
        out_specs=vmem,
        scratch_shapes=[pltpu.VMEM((devices * total, LANES), f32)],
        compiler_params=params,
        name="pack",
    )(grid, before, after)
    recv = lax.all_to_all(send, "py", 0, 0, tiled=True)

    chunk = min(256, slots)
    vel_next, back = particle_call(
        (width, devices, planes, subs_x, subs_y, slots, chunk),
        counts, recv, part_vel, part_frac, stokes_time, cells,
    )
    pencil = lax.all_to_all(back, "py", 0, 0, tiled=True)

    dep, low, high = pl.pallas_call(
        functools.partial(gather_kernel, dims),
        out_shape=(
            jax.ShapeDtypeStruct((planes * COMPS * width, length), f32),
            jax.ShapeDtypeStruct((planes * COMPS, length), bf16),
            jax.ShapeDtypeStruct((planes * COMPS, length), bf16),
        ),
        in_specs=[vmem],
        out_specs=(vmem,) * 3,
        scratch_shapes=[pltpu.VMEM((devices, total, LANES), f32)],
        compiler_params=params,
        name="gather",
    )(pencil)
    from_low = lax.ppermute(high, "px", up)
    from_high = lax.ppermute(low, "px", down)
    taps_high, taps_low = filter_blocks(length, 256)
    out = pl.pallas_call(
        functools.partial(filter_kernel, dims),
        out_shape=jax.ShapeDtypeStruct(grid.shape, f32),
        in_specs=[vmem] * 6,
        out_specs=vmem,
        scratch_shapes=[pltpu.VMEM((planes * COMPS * width, length), f32)],
        compiler_params=params,
        name="filter",
    )(grid, dep, from_low, from_high, jnp.asarray(taps_high), jnp.asarray(taps_low))
    out = out.reshape(COMPS * width, devices, planes, LANES).transpose(0, 2, 1, 3)
    return out.reshape(fluid.shape), vel_next


def solution(mesh):
    placed = (
        P(None, "px", "py", None),
        P(None, "px", "py", None),
        P(None, "px", "py", None),
        P("px", "py", None),
        P("px", "py", None),
        P("px", "py"),
    )
    return jax.shard_map(
        per_device,
        mesh=mesh,
        in_specs=placed,
        out_specs=(P(None, "px", "py", None), P(None, "px", "py", None)),
        check_vma=False,
    )
```

profile of v0, /device:TPU:1, one launch (start us, length us, event | category | flops | bytes accessed | tf_op | source)
XLA Modules:
  0.0 106.9 jit_solution(13071311159907978205)
XLA Ops:
  0.6 0.0 copy-start
  0.6 2.2 %convert.8 = bf16[3,32,2,2048]{3,2,1,0:T(2,128)(2,1)S(1)} convert(f32[3,32,2,2048]{3,2,1,0:T(2,128)} %param.8) | non-fusion elementwise | flops 393216 | bytes 2359296 | tf_op jit(solution)/shard_map/convert.5
  2.9 0.1 maximum_bitcast_fusion
  3.1 8.4 %collective-permute-start = (bf16[6,2048]{1,0:T(8,128)(2,1)S(1)}, bf16[6,2048]{1,0:T(8,128)(2,1)S(1)}, u32[]{:S(2)}, u32[]{:S(2)}) collective-permute-start(bf16[6,2048]{1,0:T(8,128)(2,1)S(1)} %squeeze.6), channel_id=1, source_target_pairs={{0,16},{16,32},{32,48},{48,64},{64,80},{80,96},{96,112},{112,128},... | collective-permute-start | bytes 73736 | tf_op jit(solution)/shard_map/ppermute | solution.py:416
  11.5 0.1 collective-permute-start.1
  11.6 1.1 collective-permute-done.before_ref
  12.6 6.2 %collective-permute-done.1.after_ref = bf16[6,2048]{1,0:T(8,128)(2,1)S(1)} collective-permute-done((bf16[6,2048]{1,0:T(8,128)(2,1)S(1)}, bf16[6,2048]{1,0:T(8,128)(2,1)S(1)}, u32[]{:S(2)}, u32[]{:S(2)}) %collective-permute-start.1) | collective-permute-done | bytes 24608 | tf_op jit(solution)/shard_map/ppermute | solution.py:417
  18.8 0.0 copy-done
  18.8 0.0 copy-start.3
  18.8 0.0 copy-start.4
  18.8 0.0 copy-start.5
  18.8 0.0 copy-start.6
  18.8 0.0 copy-start.7
  18.9 1.4 %pack.1 = bf16[16,208,128]{2,1,0:T(8,128)(2,1)S(1)} custom-call(f32[3072,128]{1,0:T(8,128)S(1)} %bitcast.18, bf16[6,2048]{1,0:T(8,128)(2,1)S(1)} %collective-permute-done.before_ref, bf16[6,2048]{1,0:T(8,128)(2,1)S(1)} %collective-permute-done.1.after_ref), custom_call_target="tpu_custom_call" | custom-call | tf_op jit(solution)/shard_map/pack/pallas_call | solution.py:421
  20.3 28.0 %all_to_all.10.recv_ref = bf16[16,208,128]{2,1,0:T(8,128)(2,1)S(1)} all-to-all(bf16[16,208,128]{2,1,0:T(8,128)(2,1)S(1)} %pack.1), channel_id=1, replica_groups=mesh['px'=16,'py'=16] {'py'}, dimensions={0} | all-to-all | bytes 1703936 | tf_op jit(solution)/shard_map/all_to_all | solution.py:430
  48.3 0.0 copy-done.3
  48.3 0.0 copy-done.4
  48.3 0.0 copy-done.5
  48.3 0.0 copy-done.6
  48.3 0.0 copy-done.7
  48.3 15.9 %particles.1 = (f32[3,4,4,1024]{3,2,1,0:T(4,128)}, bf16[16,208,128]{2,1,0:T(8,128)(2,1)S(1)}) custom-call(s32[4,4]{1,0:T(4,128)S(1)} %copy-done.7, bf16[16,208,128]{2,1,0:T(8,128)(2,1)S(1)} %all_to_all.10.recv_ref, f32[3,4,4,1024]{3,2,1,0:T(4,128)S(1)} %copy-done.3, f32[3,4,4,1024]{3,2,1,0:T(4,128)S(1)} %copy-done.4, f32[4,4,1024]{2,1,0:T(4,128)S(1)} %copy-done.5, ...), custom_call_target="tpu_custom_call" | custom-call | tf_op jit(solution)/shard_map/particles/pallas_call | solution.py:288
  64.2 0.0 copy-start.1
  64.3 0.0 copy-start.2
  64.3 25.7 %all_to_all.11.recv_ref = bf16[16,208,128]{2,1,0:T(8,128)(2,1)S(1)} all-to-all(bf16[16,208,128]{2,1,0:T(8,128)(2,1)S(1)} %get-tuple-element.7), channel_id=1, replica_groups=mesh['px'=16,'py'=16] {'py'}, dimensions={0} | all-to-all | bytes 1703936 | tf_op jit(solution)/shard_map/all_to_all | solution.py:437
  89.9 0.5 gather.1
  90.4 3.8 %collective-permute-start.2 = (bf16[6,2048]{1,0:T(8,128)(2,1)S(1)}, bf16[6,2048]{1,0:T(8,128)(2,1)S(1)}, u32[]{:S(2)}, u32[]{:S(2)}) collective-permute-start(bf16[6,2048]{1,0:T(8,128)(2,1)S(1)} %get-tuple-element.9), channel_id=1, source_target_pairs={{0,16},{16,32},{32,48},{48,64},{64,80},{80,96},{96,112},{112,128},... | collective-permute-start | bytes 73736 | tf_op jit(solution)/shard_map/ppermute | solution.py:452
  94.2 0.0 collective-permute-start.3
  94.2 1.0 collective-permute-done.2.from_low_ref
  95.2 6.2 %collective-permute-done.3.from_high_ref = bf16[6,2048]{1,0:T(8,128)(2,1)S(1)} collective-permute-done((bf16[6,2048]{1,0:T(8,128)(2,1)S(1)}, bf16[6,2048]{1,0:T(8,128)(2,1)S(1)}, u32[]{:S(2)}, u32[]{:S(2)}) %collective-permute-start.3) | collective-permute-done | bytes 24608 | tf_op jit(solution)/shard_map/ppermute | solution.py:453
  101.4 0.0 copy-done.1
  101.4 0.0 copy-done.2
  101.4 5.4 %filter.1 = f32[3072,128]{1,0:T(8,128)} custom-call(f32[3072,128]{1,0:T(8,128)S(1)} %bitcast.19, f32[192,2048]{1,0:T(8,128)S(1)} %get-tuple-element.8.dep_ref, bf16[6,2048]{1,0:T(8,128)(2,1)S(1)} %collective-permute-done.2.from_low_ref, bf16[6,2048]{1,0:T(8,128)(2,1)S(1)} %collective-permute-done.3.from_high_ref, bf16[2,4,256,256]{3,2,1,0:T(8,128)(2,1)S(1)} %copy-done.2, ...), custom_call_target="tpu_custom_call" | custom-call | tf_op jit(solution)/shard_map/filter/pallas_call | solution.py:455
  (6 shorter events, 0.2 us)
Async XLA Ops:
  0.6 18.2 %copy-start = (f32[3,32,2,2048]{3,2,1,0:T(2,128)S(1)}, f32[3,32,2,2048]{3,2,1,0:T(2,128)}, u32[]{:S(2)}) copy-start(f32[3,32,2,2048]{3,2,1,0:T(2,128)} %param.8) | copy-start | bytes 4718596
  3.1 9.6 %collective-permute-start = (bf16[6,2048]{1,0:T(8,128)(2,1)S(1)}, bf16[6,2048]{1,0:T(8,128)(2,1)S(1)}, u32[]{:S(2)}, u32[]{:S(2)}) collective-permute-start(bf16[6,2048]{1,0:T(8,128)(2,1)S(1)} %squeeze.6), channel_id=1, source_target_pairs={{0,16},{16,32},{32,48},{48,64},{64,80},{80,96},{96,112},{112,128},... | collective-permute-start | bytes 73736 | tf_op jit(solution)/shard_map/ppermute | solution.py:416
  11.5 7.3 %collective-permute-start.1 = (bf16[6,2048]{1,0:T(8,128)(2,1)S(1)}, bf16[6,2048]{1,0:T(8,128)(2,1)S(1)}, u32[]{:S(2)}, u32[]{:S(2)}) collective-permute-start(bf16[6,2048]{1,0:T(8,128)(2,1)S(1)} %squeeze.7), channel_id=1, source_target_pairs={{16,0},{32,16},{48,32},{64,48},{80,64},{96,80},{112,96},{128,112},... | collective-permute-start | bytes 73736 | tf_op jit(solution)/shard_map/ppermute | solution.py:417
  18.8 29.5 %copy-start.3 = (f32[3,4,4,1024]{3,2,1,0:T(4,128)S(1)}, f32[3,4,4,1024]{3,2,1,0:T(4,128)}, u32[]{:S(2)}) copy-start(f32[3,4,4,1024]{3,2,1,0:T(4,128)} %vel_ref.1) | copy-start | bytes 589828
  18.8 29.5 %copy-start.4 = (f32[3,4,4,1024]{3,2,1,0:T(4,128)S(1)}, f32[3,4,4,1024]{3,2,1,0:T(4,128)}, u32[]{:S(2)}) copy-start(f32[3,4,4,1024]{3,2,1,0:T(4,128)} %frac_ref.1) | copy-start | bytes 589828
  18.8 29.5 %copy-start.5 = (f32[4,4,1024]{2,1,0:T(4,128)S(1)}, f32[4,4,1024]{2,1,0:T(4,128)}, u32[]{:S(2)}) copy-start(f32[4,4,1024]{2,1,0:T(4,128)} %tau_ref.1) | copy-start | bytes 196612
  18.8 29.5 %copy-start.6 = (s32[4,4,1024]{2,1,0:T(4,128)S(1)}, s32[4,4,1024]{2,1,0:T(4,128)}, u32[]{:S(2)}) copy-start(s32[4,4,1024]{2,1,0:T(4,128)} %cells_ref.1) | copy-start | bytes 196612
  18.8 29.5 %copy-start.7 = (s32[4,4]{1,0:T(4,128)S(1)}, s32[4,4]{1,0:T(4,128)}, u32[]{:S(2)}) copy-start(s32[4,4]{1,0:T(4,128)} %counts_ref.1) | copy-start | bytes 196
  64.2 37.2 %copy-start.1 = (bf16[2,4,256,256]{3,2,1,0:T(8,128)(2,1)S(1)}, bf16[2,4,256,256]{3,2,1,0:T(8,128)(2,1)}, u32[]{:S(2)}) copy-start(bf16[2,4,256,256]{3,2,1,0:T(8,128)(2,1)} %constant.5.clone.low_ref) | copy-start | bytes 3145732
  64.3 37.2 %copy-start.2 = (bf16[2,4,256,256]{3,2,1,0:T(8,128)(2,1)S(1)}, bf16[2,4,256,256]{3,2,1,0:T(8,128)(2,1)}, u32[]{:S(2)}) copy-start(bf16[2,4,256,256]{3,2,1,0:T(8,128)(2,1)} %constant.4.clone.high_ref) | copy-start | bytes 3145732
  90.4 4.8 %collective-permute-start.2 = (bf16[6,2048]{1,0:T(8,128)(2,1)S(1)}, bf16[6,2048]{1,0:T(8,128)(2,1)S(1)}, u32[]{:S(2)}, u32[]{:S(2)}) collective-permute-start(bf16[6,2048]{1,0:T(8,128)(2,1)S(1)} %get-tuple-element.9), channel_id=1, source_target_pairs={{0,16},{16,32},{32,48},{48,64},{64,80},{80,96},{96,112},{112,128},... | collective-permute-start | bytes 73736 | tf_op jit(solution)/shard_map/ppermute | solution.py:452
  94.2 7.2 %collective-permute-start.3 = (bf16[6,2048]{1,0:T(8,128)(2,1)S(1)}, bf16[6,2048]{1,0:T(8,128)(2,1)S(1)}, u32[]{:S(2)}, u32[]{:S(2)}) collective-permute-start(bf16[6,2048]{1,0:T(8,128)(2,1)S(1)} %get-tuple-element.10), channel_id=1, source_target_pairs={{16,0},{32,16},{48,32},{64,48},{80,64},{96,80},{112,96},{128,112},... | collective-permute-start | bytes 73736 | tf_op jit(solution)/shard_map/ppermute | solution.py:453
where the time goes:
time: 107 us
  blocking collectives  53.7 us (50%)
  Pallas kernels  23.3 us (22%)
  waiting for transfers between devices  14.5 us (14%)
  starting transfers between devices  12.2 us (11%)
  other arithmetic  2.26 us (2%)
    all_to_all x1, blocking collectives, per_device(): recv = lax.all_to_all(send, 'py', 0, 0, tiled=True)  28 us
    all_to_all x1, blocking collectives, per_device(): pencil = lax.all_to_all(back, 'py', 0, 0, tiled=True)  25.7 us
    pallas_call x1, Pallas kernels, particle_call(): pl.pallas_call(functools.partial(particle_kernel, dims), out_shape=(jax.S...  15.9 us
    ppermute x1, starting transfers between devices, per_device(): before = lax.ppermute(edges[1], 'px', up)  8.38 us
    ppermute x1, waiting for transfers between devices, per_device(): from_high = lax.ppermute(low, 'px', down)  6.22 us
    ppermute x1, waiting for transfers between devices, per_device(): after = lax.ppermute(edges[0], 'px', down)  6.17 us
    pallas_call x1, Pallas kernels, per_device(): pl.pallas_call(functools.partial(filter_kernel, dims), out_shape=jax.Shap...  5.44 us
    ppermute x1, starting transfers between devices, per_device(): from_low = lax.ppermute(high, 'px', up)  3.76 us
  transfers between devices with their start and end apart: 4, of which 4 were waited for; matrix products, arithmetic and copies ran while one was open for 0% of the time, Pallas kernels for 0%

commit v1 on v0

v1 whole, which is shorter than its diff:
```python
import functools
import math

import jax
import jax.numpy as jnp
import numpy as np
from jax import lax
from jax.experimental import pallas as pl
from jax.experimental.pallas import tpu as pltpu
from jax.sharding import PartitionSpec as P

mass_load = 4.0
step_dt = 0.5
viscous_step = 0.25
forcing_gain = 1.5
forced_modes = 4

COMPS = 3
LANES = 128
VMEM_LIMIT = 24 * 1024 * 1024
VMEM_MOST = 58 * 1024 * 1024
f32 = jnp.float32
bf16 = jnp.bfloat16
NT = (((1,), (1,)), ((), ()))


def filter_blocks(length, width):
    k = np.fft.fftfreq(length, 1.0 / length)
    angle = 2.0 * math.pi * k / length
    gain = np.exp(-viscous_step * angle * angle)
    gain = gain * np.where((abs(k) >= 1) & (abs(k) <= forced_modes), 1.0 + forcing_gain, 1.0)
    taps = np.fft.ifft(gain).real
    blocks = length // width
    half = blocks // 2
    inner = np.arange(width)
    full = []
    for d in range(blocks):
        full.append(taps[(width * d + inner[None, :] - inner[:, None]) % length])
    sums = np.stack([0.5 * (full[d] + full[d + half]) for d in range(half)])
    diffs = np.stack([0.5 * (full[d] - full[d + half]) for d in range(half)])
    both = np.stack([sums, diffs]).astype(np.float32)
    high = both.astype(jnp.bfloat16)
    low = (both - high.astype(np.float32)).astype(jnp.bfloat16)
    return high, low


def side_picker():
    row_id = lax.broadcasted_iota(jnp.int32, (8, LANES), 0)
    lane_id = lax.broadcasted_iota(jnp.int32, (8, LANES), 1)
    pick = ((row_id == 0) & (lane_id == LANES - 1)) | ((row_id == 1) & (lane_id == 0))
    return jnp.where(pick, 1.0, 0.0).astype(bf16)


def pack_kernel(dims, pieces, grid_hbm, out_ref, msg, held, sems):
    width, devices, planes = dims
    depth = devices * planes
    count = sum(n for _, n in pieces)
    rows = COMPS * count
    used = planes * rows
    total = out_ref.shape[1]
    copies = []
    for c in range(COMPS):
        off = c * count
        for x, n in pieces:
            copy = pltpu.make_async_copy(
                grid_hbm.at[pl.ds((c * width + x) * depth, n * depth), :],
                held.at[pl.ds(off * depth, n * depth), :],
                sems.at[len(copies)],
            )
            copy.start()
            copies.append(copy)
            off += n
    pick = side_picker()
    for j in range(devices):
        msg[pl.ds(j * total + used, total - used), :] = jnp.zeros((total - used, LANES), f32)
    for c in range(COMPS):
        for i in range(len(pieces)):
            copies[c * len(pieces) + i].wait()
        for j in range(devices):
            for p in range(planes):
                msg[pl.ds(j * total + p * rows + c * count, count), :] = held[
                    pl.ds(c * count * depth + j * planes + p, count, stride=depth), :
                ]
    for j in range(devices):
        for p in range(planes):
            block = msg[pl.ds(j * total + p * rows, rows), :].astype(bf16)
            edge = lax.dot_general(pick, block, NT, preferred_element_type=f32)
            right = (j + 1) % devices
            left = (j - 1) % devices
            msg[pl.ds(right * total + used + 2 * p, 1), 0:rows] = edge[0:1]
            msg[pl.ds(left * total + used + 2 * p + 1, 1), 0:rows] = edge[1:2]
    for j in range(devices):
        out_ref[j] = msg[pl.ds(j * total, total), :].astype(bf16)


def edge_kernel(planes, count, recv_ref, low_ref, high_ref, msg, out):
    devices = recv_ref.shape[0]
    used = planes * COMPS * count
    lines = planes * COMPS
    for s in range(devices):
        msg[...] = recv_ref[s].astype(f32)
        for e in range(lines):
            for side in range(2):
                at = e * count + side * (count - 1)
                out[side, pl.ds(s * lines + e, 1), :] = msg[pl.ds(at, 1), :]
        for side in range(2):
            out[side, pl.ds(devices * lines + s * 2 * planes, 2 * planes), :] = msg[pl.ds(used, 2 * planes), :]
    low_ref[...] = out[0].astype(bf16)
    high_ref[...] = out[1].astype(bf16)


def lane_of_x(local, c, count, ghosts):
    if not ghosts:
        return c * count + local
    lane = c * count + local - 1
    lane = jnp.where(local == 0, LANES // 2 + c * count + count - 1, lane)
    return jnp.where(local == count + 1, LANES // 2 + c * count, lane)


def same_cell(c, count, ghosts, depth, rows):
    local = lax.broadcasted_iota(jnp.int32, (rows, LANES), 0) // depth
    col = lax.broadcasted_iota(jnp.int32, (rows, LANES), 1)
    return jnp.where(col == lane_of_x(local, c, count, ghosts), 1.0, 0.0).astype(bf16)


def side_lane(depth, shape, dim):
    ghost = lax.broadcasted_iota(jnp.int32, shape, dim)
    lane = lax.broadcasted_iota(jnp.int32, shape, 1 - dim)
    hit = ((ghost < depth) & (lane == LANES - 1)) | ((ghost >= depth) & (lane == 0))
    return jnp.where(hit, 1.0, 0.0).astype(bf16)


def particle_kernel(dims, plan, *refs):
    width, devices, planes, subs_x, subs_y, slots, chunk = dims
    count, moves, ghosts, starts, strips, writes_all = plan
    counts_ref, recv_ref, vel_ref, frac_ref, tau_ref, cells_ref = refs[:6]
    refs = refs[6:]
    if ghosts:
        before_ref, after_ref = refs[:2]
        refs = refs[2:]
    if writes_all:
        other_ref = refs[0]
        refs = refs[1:]
    vel_out_ref, send_ref, msg, rows_buf, ghost, field, deposit, prep, ints = refs
    held = count + 2 if ghosts else count
    depth = devices * planes
    tile_x = width // subs_x
    tile_y = LANES // subs_y
    total = recv_ref.shape[1]
    rows = COMPS * count
    used = planes * rows
    cells = held * depth
    near = 4
    pair = 2 * depth
    pairs = tile_x // 2
    strip_rows = tile_x * depth
    core = len(starts) * strip_rows
    block = near * depth

    if writes_all:
        others = [a for a in range(subs_x) if a not in strips]
        for c in range(COMPS):
            for i, a in enumerate(others):
                vel_out_ref[c, a] = other_ref[c, i]

    lines = planes * COMPS
    for s in range(devices):
        msg[pl.ds(0, total), :] = recv_ref[s].astype(f32)
        for p in range(planes):
            z = s * planes + p
            for c in range(COMPS):
                for off, n, local in moves:
                    rows_buf[pl.ds(c * cells + local * depth + z, n, stride=depth), :] = msg[
                        pl.ds(p * rows + c * count + off, n), :
                    ]
            ghost[pl.ds(z, 1), :] = msg[pl.ds(used + 2 * p, 1), :]
            ghost[pl.ds(depth + z, 1), :] = msg[pl.ds(used + 2 * p + 1, 1), :]
    if ghosts:
        lane8 = lax.broadcasted_iota(jnp.int32, (2 * depth, LANES), 1)
        for side, ref in enumerate((before_ref, after_ref)):
            msg[pl.ds(0, ref.shape[0]), :] = ref[...].astype(f32)
            for s in range(devices):
                for p in range(planes):
                    z = s * planes + p
                    for c in range(COMPS):
                        at = c * cells + side * (held - 1) * depth + z
                        rows_buf[pl.ds(at, 1), :] = msg[pl.ds(s * lines + p * COMPS + c, 1), :]
            turned = []
            for lr in range(2):
                turned.append(msg[pl.ds(devices * lines + lr, depth, stride=2), :])
            turned = jnp.roll(jnp.concatenate(turned, axis=0), LANES // 2, axis=1)
            wanted = (lane8 - LANES // 2) % count == (count - 1 if side == 0 else 0)
            ghost[...] = jnp.where((lane8 >= LANES // 2) & wanted, turned, ghost[...])
    own_z = lax.broadcasted_iota(jnp.int32, (cells, 2 * depth), 0) % depth
    own_z = own_z == lax.broadcasted_iota(jnp.int32, (cells, 2 * depth), 1) % depth
    lane = lax.broadcasted_iota(jnp.int32, (cells, LANES), 1)
    strip_lane = lane[:strip_rows]
    for c in range(COMPS):
        at = pl.ds(c * cells, cells)
        wide = lax.dot_general(
            same_cell(c, count, ghosts, depth, cells), ghost[...].astype(bf16), NT, preferred_element_type=f32
        )
        wide = jnp.where(own_z, wide, 0.0).astype(bf16)
        outer = jnp.dot(wide, side_lane(depth, (2 * depth, LANES), 0), preferred_element_type=f32)
        inner = rows_buf[at, :]
        lower = jnp.where(lane == LANES - 1, outer, inner)
        upper = jnp.where(lane == 0, outer, inner)
        for side, value in enumerate((lower, upper)):
            moved = jnp.roll(value, LANES // 2, axis=1)
            for b in range(side * subs_y // 2, (side + 1) * subs_y // 2):
                first_half = (strip_lane - (b * tile_y - 16)) % LANES < LANES // 2
                for k, start in enumerate(starts):
                    r = start * depth
                    field[b, pl.ds(c * core + k * strip_rows, strip_rows), :] = jnp.where(
                        first_half, value[r : r + strip_rows], moved[r + pair : r + pair + strip_rows]
                    ).astype(bf16)

    x_rows = lax.broadcasted_iota(jnp.int32, (8, chunk), 0)
    z_rows = lax.broadcasted_iota(jnp.int32, (depth, chunk), 0)
    y_rows = lax.broadcasted_iota(jnp.int32, (tile_y + 16, chunk), 0) - 8

    def strip(k, carry):
        a = strips[0] + k * (strips[1] - strips[0])
        place_a = k if not writes_all else a
        for d in range(COMPS):
            f = frac_ref[d, a]
            prep[3 * d] = 0.5 * (0.5 - f) ** 2
            prep[3 * d + 1] = 0.75 - f * f
            prep[3 * d + 2] = 0.5 * (0.5 + f) ** 2
        prep[9] = step_dt / tau_ref[a]
        cell = cells_ref[a]
        ints[0] = cell // (tile_y * depth)
        ints[1] = cell // depth % tile_y
        ints[2] = cell % depth
        first = k * strip_rows

        for b in range(subs_y):
            filled = counts_ref[a, b]
            blocks = tile_x * depth // block
            data = jnp.concatenate(
                [
                    jnp.concatenate(
                        [
                            field[b, pl.ds(pl.multiple_of(c * core + first + t * block, block), block), :]
                            for t in range(blocks)
                        ],
                        axis=1,
                    )
                    for c in range(COMPS)
                ],
                axis=0,
            )
            acc = None
            for start in range(0, slots, chunk):
                at = slice(start, start + chunk)
                row = lambda i: prep[i, b : b + 1, at]
                xc, yc, zc = (ints[i, b : b + 1, at] for i in range(3))
                here = lax.broadcasted_iota(jnp.int32, (1, chunk), 1) + start < filled
                dx = x_rows - (xc & 1)
                wx = jnp.where(
                    dx == 0, row(0), jnp.where(dx == 1, row(1), jnp.where(dx == 2, row(2), 0.0))
                )
                dy = y_rows - yc
                y_low, y_mid, y_high = (jnp.where(here, row(3 + i), 0.0) for i in range(3))
                wy = jnp.where(
                    dy == -1, y_low, jnp.where(dy == 0, y_mid, jnp.where(dy == 1, y_high, 0.0))
                )
                dz = (z_rows - zc + 1) & (depth - 1)
                wz = jnp.where(
                    dz == 0, row(6), jnp.where(dz == 1, row(7), jnp.where(dz == 2, row(8), 0.0))
                )
                groups = LANES // 8
                half_groups = groups // 2
                blank = jnp.zeros((8, chunk), f32)
                pieces = [blank] * (groups * blocks)
                for q in range(pairs):
                    chosen = xc >> 1 == q
                    for g in range(tile_y // 8 + 2):
                        place = (b * tile_y // 8 - 1 + g + (q % 2) * half_groups) % groups
                        pieces[q // 2 * groups + place] = jnp.where(chosen, wy[8 * g : 8 * g + 8], 0.0)
                wy = jnp.concatenate(pieces, axis=0).astype(bf16)
                raw = jnp.dot(data, wy, preferred_element_type=f32)
                rate = row(9)
                shares = []
                for c in range(COMPS):
                    found = None
                    for i in range(near):
                        part = None
                        for g in range(depth // 8):
                            at8 = c * block + i * depth + 8 * g
                            term = raw[at8 : at8 + 8] * wz[8 * g : 8 * g + 8]
                            part = term if part is None else part + term
                        part = part * wx[i : i + 1]
                        found = part if found is None else found + part
                    interp = jnp.sum(found, axis=0, keepdims=True)
                    velocity = vel_ref[c, a, b : b + 1, at]
                    change = rate * (interp - velocity)
                    vel_out_ref[c, place_a, b : b + 1, at] = jnp.where(here, velocity + change, velocity)
                    pull = jnp.where(here, -mass_load * change, 0.0) * wx
                    shares = shares + [(pull[i : i + 1] * wz).astype(bf16) for i in range(near)]
                part = lax.dot_general(
                    jnp.concatenate(shares, axis=0), wy, NT, preferred_element_type=f32
                )
                acc = part if acc is None else acc + part
            for c in range(COMPS):
                for t in range(blocks):
                    base = pl.multiple_of(c * core + first + t * block, block)
                    deposit[b, pl.ds(base, block), :] = acc[
                        c * block : (c + 1) * block, t * LANES : (t + 1) * LANES
                    ]
        return carry

    lax.fori_loop(0, len(strips), strip, 0)

    gathered = jnp.zeros((2 * depth, LANES), f32)
    empty = jnp.zeros((pair, LANES), f32)
    for c in range(COMPS):
        at = pl.ds(c * cells, cells)
        sides = []
        for side in range(2):
            found = []
            for k in range(len(starts)):
                even = odd = None
                for b in range(side * subs_y // 2, (side + 1) * subs_y // 2):
                    value = deposit[b, pl.ds(c * core + k * strip_rows, strip_rows), :]
                    first_half = (strip_lane - (b * tile_y - 16)) % LANES < LANES // 2
                    one = jnp.where(first_half, value, 0.0)
                    two = jnp.where(first_half, 0.0, value)
                    even = one if even is None else even + one
                    odd = two if odd is None else odd + two
                moved = jnp.roll(odd, LANES // 2, axis=1)
                found.append(
                    jnp.concatenate([even, empty], axis=0) + jnp.concatenate([empty, moved], axis=0)
                )
            shared = strip_rows + pair - (starts[1] - starts[0]) * depth
            if shared == 0:
                sides.append(jnp.concatenate(found, axis=0))
            else:
                keep = strip_rows + pair - shared
                middle = found[0][keep:] + found[1][:shared]
                sides.append(jnp.concatenate([found[0][:keep], middle, found[1][shared:]], axis=0))
        lower, upper = sides
        first_lane = lane == 0
        last_lane = lane == LANES - 1
        rows_buf[at, :] = jnp.where(last_lane, 0.0, lower) + jnp.where(first_lane, 0.0, upper)
        outer = jnp.where(last_lane, lower, jnp.where(first_lane, upper, 0.0)).astype(bf16)
        wide = jnp.dot(outer, side_lane(depth, (LANES, 2 * depth), 1), preferred_element_type=f32)
        wide = jnp.where(own_z, wide, 0.0).astype(bf16)
        gathered = gathered + lax.dot_general(
            wide, same_cell(c, held, False, depth, cells), (((0,), (0,)), ((), ())), preferred_element_type=f32
        )
    ghost[...] = gathered
    rows = COMPS * held
    used = planes * rows
    total = send_ref.shape[1]
    for s in range(devices):
        if total > used + 2 * planes:
            msg[pl.ds(used, total - used), :] = jnp.zeros((total - used, LANES), f32)
        for p in range(planes):
            z = s * planes + p
            for c in range(COMPS):
                msg[pl.ds(p * rows + c * held, held), :] = rows_buf[
                    pl.ds(c * cells + z, held, stride=depth), :
                ]
            msg[pl.ds(used + 2 * p, 1), :] = ghost[pl.ds(z, 1), :]
            msg[pl.ds(used + 2 * p + 1, 1), :] = ghost[pl.ds(depth + z, 1), :]
        send_ref[s] = msg[pl.ds(0, total), :].astype(bf16)


def particle_call(dims, plan, counts, recv, part_vel, part_frac, stokes_time, cells, extra):
    width, devices, planes, subs_x, subs_y, slots, chunk = dims
    count, moves, ghosts, starts, strips, writes_all = plan
    vmem = pl.BlockSpec(memory_space=pltpu.VMEM)
    held = count + 2 if ghosts else count
    depth = devices * planes
    total_out = message_rows(planes, held)
    core_rows = COMPS * len(strips) * (width // subs_x) * depth
    vel_shape = part_vel.shape if writes_all else (COMPS, len(strips), subs_y, slots)
    return pl.pallas_call(
        functools.partial(particle_kernel, dims, plan),
        out_shape=(
            jax.ShapeDtypeStruct(vel_shape, f32),
            jax.ShapeDtypeStruct((devices, total_out, LANES), bf16),
        ),
        in_specs=[pl.BlockSpec(memory_space=pltpu.SMEM)] + [vmem] * (5 + len(extra)),
        out_specs=(vmem, vmem),
        scratch_shapes=[
            pltpu.VMEM((devices * planes * 5, LANES), f32),
            pltpu.VMEM((COMPS * held * depth + 8 * depth, LANES), f32),
            pltpu.VMEM((2 * depth, LANES), f32),
            pltpu.VMEM((subs_y, core_rows, LANES), bf16),
            pltpu.VMEM((subs_y, core_rows, LANES), f32),
            pltpu.VMEM((10, subs_y, slots), f32),
            pltpu.VMEM((3, subs_y, slots), jnp.int32),
        ],
        compiler_params=pltpu.CompilerParams(vmem_limit_bytes=VMEM_LIMIT),
        cost_estimate=pl.CostEstimate(flops=int(8e9), bytes_accessed=int(2e7), transcendentals=0),
        name="particles_outer" if ghosts else "particles_inner",
    )(counts, recv, part_vel, part_frac, stokes_time, cells, *extra)


def gather_kernel(planes, held, skip, recv_ref, out_ref, *refs):
    msg = refs[-1]
    rows = COMPS * held
    used = planes * rows
    count = recv_ref.shape[0]
    inner = held - 2 * skip
    for j in range(count):
        msg[j] = recv_ref[j].astype(f32)
    place = side_picker()
    for j in range(count):
        left = (j - 1) % count
        right = (j + 1) % count
        lanes = slice(j * LANES, (j + 1) * LANES)
        lows, highs = [], []
        for p in range(planes):
            pair = jnp.concatenate(
                [
                    msg[right, used + 2 * p : used + 2 * p + 1, :],
                    msg[left, used + 2 * p + 1 : used + 2 * p + 2, :],
                    jnp.zeros((6, LANES), f32),
                ],
                axis=0,
            ).astype(bf16)
            added = lax.dot_general(
                pair, place, (((0,), (0,)), ((), ())), preferred_element_type=f32
            )
            block = msg[j, p * rows : (p + 1) * rows, :] + added[:rows]
            for c in range(COMPS):
                e = p * COMPS + c
                at = c * held
                lows.append(block[at : at + 1])
                highs.append(block[at + held - 1 : at + held])
                out_ref[pl.ds(e * inner, inner), lanes] = block[at + skip : at + skip + inner]
        if skip:
            refs[0][:, lanes] = jnp.concatenate(lows, axis=0).astype(bf16)
            refs[1][:, lanes] = jnp.concatenate(highs, axis=0).astype(bf16)


def gather_call(planes, held, skip, recv):
    devices = recv.shape[0]
    length = devices * LANES
    vmem = pl.BlockSpec(memory_space=pltpu.VMEM)
    lines = planes * COMPS
    shapes = [jax.ShapeDtypeStruct((lines * (held - 2 * skip), length), f32)]
    if skip:
        shapes += [jax.ShapeDtypeStruct((lines, length), bf16)] * 2
    return pl.pallas_call(
        functools.partial(gather_kernel, planes, held, skip),
        out_shape=tuple(shapes),
        in_specs=[vmem],
        out_specs=(vmem,) * len(shapes),
        scratch_shapes=[pltpu.VMEM(recv.shape, f32)],
        compiler_params=pltpu.CompilerParams(vmem_limit_bytes=VMEM_LIMIT),
        cost_estimate=pl.CostEstimate(flops=int(1e8), bytes_accessed=int(2e6), transcendentals=0),
        name="gather",
    )(recv)


def filter_kernel(
    dims, outer_pieces, inner_piece, grid_ref, outer_ref, inner_ref, from_low_ref, from_high_ref,
    high_ref, low_ref, out_ref, mixed, dep,
):
    width, devices, planes = dims
    depth = devices * planes
    outer_count = sum(n for _, n in outer_pieces)
    inner_x, inner_count = inner_piece
    for p in range(planes):
        for c in range(COMPS):
            e = p * COMPS + c
            dep[...] = jnp.zeros(dep.shape, f32)
            off = e * outer_count
            for x, n in outer_pieces:
                dep[pl.ds(x, n), :] = outer_ref[pl.ds(off, n), :]
                off += n
            dep[pl.ds(inner_x, inner_count), :] += inner_ref[pl.ds(e * inner_count, inner_count), :]
            dep[pl.ds(0, 1), :] += from_low_ref[e : e + 1, :].astype(f32)
            dep[pl.ds(width - 1, 1), :] += from_high_ref[e : e + 1, :].astype(f32)
            for j in range(devices):
                lanes = slice(j * LANES, (j + 1) * LANES)
                fluid = grid_ref[pl.ds(c * width * depth + j * planes + p, width, stride=depth), :]
                mixed[pl.ds(e * width, width), lanes] = fluid + dep[0:width, lanes].astype(bf16).astype(f32)
    folds = high_ref.shape[1]
    block = high_ref.shape[2]
    sides = []
    for sign in range(2):
        highs, lows = [], []
        for i in range(folds):
            one = mixed[:, i * block : (i + 1) * block]
            two = mixed[:, (i + folds) * block : (i + folds + 1) * block]
            value = one + two if sign == 0 else one - two
            high = value.astype(bf16)
            highs.append(high)
            lows.append((value - high.astype(f32)).astype(bf16))
        sides.append((highs, lows))
    for o in range(folds):
        results = []
        for sign in range(2):
            highs, lows = sides[sign]
            sums = {1: None, -1: None}
            for i in range(folds):
                d = (o - i) % folds
                key = -1 if sign == 1 and o < i else 1
                part = jnp.dot(highs[i], high_ref[sign, d], preferred_element_type=f32)
                part = part + jnp.dot(lows[i], high_ref[sign, d], preferred_element_type=f32)
                part = part + jnp.dot(highs[i], low_ref[sign, d], preferred_element_type=f32)
                sums[key] = part if sums[key] is None else sums[key] + part
            results.append(sums[1] if sums[-1] is None else sums[1] - sums[-1])
        for flip in range(2):
            value = results[0] + results[1] if flip == 0 else results[0] - results[1]
            for half in range(block // LANES):
                j = (o + flip * folds) * (block // LANES) + half
                for p in range(planes):
                    for c in range(COMPS):
                        e = p * COMPS + c
                        out_ref[pl.ds(c * width * depth + j * planes + p, width, stride=depth), :] = value[
                            e * width : (e + 1) * width, half * LANES : (half + 1) * LANES
                        ]


def message_rows(planes, held):
    return -(-(planes * COMPS * held + 2 * planes) // 16) * 16


def exchange(low, high):
    size = lax.axis_size("px")
    even = lax.axis_index("px") % 2 == 0
    first = [(i, i ^ 1) for i in range(size)]
    second = [(i, (i + 1) % size if i % 2 else (i - 1) % size) for i in range(size)]
    far = lax.ppermute(jnp.where(even, low, high), "px", second)
    close = lax.ppermute(jnp.where(even, high, low), "px", first)
    return jnp.where(even, far, close), jnp.where(even, close, far)


def per_device(fluid, part_vel, part_frac, stokes_time, cells, counts):
    devices = lax.axis_size("py")
    _, width, planes, length = fluid.shape
    subs_x, subs_y, slots = stokes_time.shape
    depth = planes * devices
    tile_x = width // subs_x
    params = pltpu.CompilerParams(vmem_limit_bytes=VMEM_LIMIT)
    vmem = pl.BlockSpec(memory_space=pltpu.VMEM)
    dims = (width, devices, planes)

    outer = ((0, tile_x + 1), (width - tile_x - 1, tile_x + 1))
    inner = (tile_x - 1, width - 2 * tile_x + 2)
    outer_count = 2 * (tile_x + 1)
    inner_count = inner[1]
    grid = fluid.reshape(COMPS * width, planes, devices, LANES).transpose(0, 2, 1, 3)
    grid = grid.reshape(COMPS * width * depth, LANES)
    outer_rows = message_rows(planes, outer_count)
    inner_rows = message_rows(planes, inner_count)
    hbm = pl.BlockSpec(memory_space=pltpu.HBM)

    def pack(pieces, total, limit):
        count = sum(n for _, n in pieces)
        return pl.pallas_call(
            functools.partial(pack_kernel, dims, pieces),
            out_shape=jax.ShapeDtypeStruct((devices, total, LANES), bf16),
            in_specs=[hbm],
            out_specs=vmem,
            scratch_shapes=[
                pltpu.VMEM((devices * total, LANES), f32),
                pltpu.VMEM((COMPS * count * depth + 8 * depth, LANES), f32),
                pltpu.SemaphoreType.DMA((COMPS * len(pieces),)),
            ],
            compiler_params=pltpu.CompilerParams(vmem_limit_bytes=limit),
            cost_estimate=pl.CostEstimate(flops=int(1e8), bytes_accessed=int(2e6), transcendentals=0),
            name="pack",
        )(grid)

    send_outer = pack(outer, outer_rows, VMEM_MOST)
    send_inner = pack((inner,), inner_rows, VMEM_MOST)
    recv_outer = lax.all_to_all(send_outer, "py", 0, 0, tiled=True)
    recv_outer, send_inner = lax.optimization_barrier((recv_outer, send_inner))
    recv_inner = lax.all_to_all(send_inner, "py", 0, 0, tiled=True)

    edge_rows = devices * planes * (COMPS + 2)
    low, high = pl.pallas_call(
        functools.partial(edge_kernel, planes, outer_count),
        out_shape=(jax.ShapeDtypeStruct((edge_rows, LANES), bf16),) * 2,
        in_specs=[vmem],
        out_specs=(vmem, vmem),
        scratch_shapes=[pltpu.VMEM((outer_rows, LANES), f32), pltpu.VMEM((2, edge_rows, LANES), f32)],
        compiler_params=params,
        name="edges",
    )(recv_outer)
    before, after = exchange(low, high)

    sizes = (width, devices, planes, subs_x, subs_y, slots, min(256, slots))
    half = tile_x + 1
    outer_plan = (
        outer_count, ((0, half, 1), (half, half, half + 1)), True, (0, tile_x + 2), (0, subs_x - 1), False,
    )
    inner_plan = (inner_count, ((0, inner_count, 0),), False, (0, tile_x), (1, 2), True)
    vel_outer, back_outer = particle_call(
        sizes, outer_plan, counts, recv_outer, part_vel, part_frac, stokes_time, cells, (before, after)
    )
    pencil_outer = lax.all_to_all(back_outer, "py", 0, 0, tiled=True)
    vel_next, back_inner = particle_call(
        sizes, inner_plan, counts, recv_inner, part_vel, part_frac, stokes_time, cells, (vel_outer,)
    )
    pencil_outer, back_inner = lax.optimization_barrier((pencil_outer, back_inner))
    pencil_inner = lax.all_to_all(back_inner, "py", 0, 0, tiled=True)
    dep_outer, low, high = gather_call(planes, outer_count + 2, 1, pencil_outer)
    from_low, from_high = exchange(low, high)
    (dep_inner,) = gather_call(planes, inner_count, 0, pencil_inner)
    taps_high, taps_low = filter_blocks(length, 256)
    out = pl.pallas_call(
        functools.partial(filter_kernel, dims, outer, inner),
        out_shape=jax.ShapeDtypeStruct(grid.shape, f32),
        in_specs=[vmem] * 7,
        out_specs=vmem,
        scratch_shapes=[
            pltpu.VMEM((planes * COMPS * width, length), f32),
            pltpu.VMEM((width + 8, length), f32),
        ],
        compiler_params=params,
        name="filter",
    )(grid, dep_outer, dep_inner, from_low, from_high, jnp.asarray(taps_high), jnp.asarray(taps_low))
    out = out.reshape(COMPS * width, devices, planes, LANES).transpose(0, 2, 1, 3)
    return out.reshape(fluid.shape), vel_next


def solution(mesh):
    placed = (
        P(None, "px", "py", None),
        P(None, "px", "py", None),
        P(None, "px", "py", None),
        P("px", "py", None),
        P("px", "py", None),
        P("px", "py"),
    )
    return jax.shard_map(
        per_device,
        mesh=mesh,
        in_specs=placed,
        out_specs=(P(None, "px", "py", None), P(None, "px", "py", None)),
        check_vma=False,
    )
```

time: 107 us -> 99.1 us (0.926)
  the two profiles are of different devices: /device:TPU:1 before, /device:TPU:2 now
where the time goes in v1:
time: 99.1 us; the launch traced here: 98.5 us
  waiting for transfers between devices  37 us (37%)
  Pallas kernels  31.2 us (31%)
  starting transfers between devices  27.4 us (28%)
  local copies, waits for them, and re-layouts  1.98 us (2%)
    pallas_call x2, Pallas kernels, particle_call(): pl.pallas_call(functools.partial(particle_kernel, dims, plan), out_shape=...  19 us
    all_to_all x1, waiting for transfers between devices, per_device(): recv_outer = lax.all_to_all(send_outer, 'py', 0, 0, tiled=True)  12.3 us
    all_to_all x1, starting transfers between devices, per_device(): recv_outer = lax.all_to_all(send_outer, 'py', 0, 0, tiled=True)  8.65 us
    ppermute x2, starting transfers between devices, exchange(): far = lax.ppermute(jnp.where(even, low, high), 'px', second)  7.64 us
    all_to_all x1, waiting for transfers between devices, per_device(): pencil_outer = lax.all_to_all(back_outer, 'py', 0, 0, tiled=True)  6.78 us
    ppermute x2, waiting for transfers between devices, exchange(): far = lax.ppermute(jnp.where(even, low, high), 'px', second)  6.55 us
    pallas_call x1, Pallas kernels, per_device(): pl.pallas_call(functools.partial(filter_kernel, dims, outer, inner), out_...  5.87 us
    all_to_all x1, waiting for transfers between devices, per_device(): pencil_inner = lax.all_to_all(back_inner, 'py', 0, 0, tiled=True)  5.69 us
  transfers between devices with their start and end apart: 8, of which 6 were waited for; matrix products, arithmetic and copies ran while one was open for 0% of the time, Pallas kernels for 22%

profile of v1, /device:TPU:2, one launch (start us, length us, event | category | flops | bytes accessed | tf_op | source)
XLA Modules:
  0.0 98.5 jit_solution(8929026320783415517)
XLA Ops:
  0.6 2.6 %pack.2 = bf16[16,112,128]{2,1,0:T(8,128)(2,1)} custom-call(f32[3072,128]{1,0:T(8,128)} %bitcast.10), custom_call_target="tpu_custom_call" | custom-call | flops 100000000 | bytes 2000000 | tf_op jit(solution)/shard_map/pack/pallas_call | solution.py:557
  3.3 8.6 %all-to-all-start = ((bf16[16,112,128]{2,1,0:T(8,128)(2,1)}), bf16[16,112,128]{2,1,0:T(8,128)(2,1)S(1)}, u32[]{:S(2)}, u32[]{:S(2)}) async-start(bf16[16,112,128]{2,1,0:T(8,128)(2,1)} %pack.2), calls=%async_computation | async-start | bytes 917504 | tf_op jit(solution)/shard_map/all_to_all | solution.py:574
  11.9 0.0 copy-start.3
  11.9 0.0 copy-start.4
  11.9 0.0 copy-start.5
  12.0 0.0 copy-start.6
  12.0 0.0 copy-start.7
  12.0 2.7 %pack.3 = bf16[16,112,128]{2,1,0:T(8,128)(2,1)} custom-call(f32[3072,128]{1,0:T(8,128)} %bitcast.11), custom_call_target="tpu_custom_call" | custom-call | flops 100000000 | bytes 2000000 | tf_op jit(solution)/shard_map/pack/pallas_call | solution.py:557
  14.7 12.3 %all-to-all-done.recv_ref.refs_1_ = bf16[16,112,128]{2,1,0:T(8,128)(2,1)S(1)} async-done(((bf16[16,112,128]{2,1,0:T(8,128)(2,1)}), bf16[16,112,128]{2,1,0:T(8,128)(2,1)S(1)}, u32[]{:S(2)}, u32[]{:S(2)}) %all-to-all-start) | async-done | bytes 458784 | tf_op jit(solution)/shard_map/all_to_all | solution.py:574
  27.0 0.1 edges.1
  27.2 0.1 collective-permute-start.1
  27.3 4.6 %collective-permute-start = (bf16[160,128]{1,0:T(8,128)(2,1)S(1)}, bf16[160,128]{1,0:T(8,128)(2,1)S(1)}, u32[]{:S(2)}, u32[]{:S(2)}) collective-permute-start(bf16[160,128]{1,0:T(8,128)(2,1)S(1)} %get-tuple-element.31), channel_id=1, source_target_pairs={{0,240},{16,32},{32,16},{48,64},{64,48},{80,96},{96,80},{112,128},... | collective-permute-start | bytes 122888 | tf_op jit(solution)/shard_map/ppermute | solution.py:530
  31.8 3.6 %all-to-all-start.2 = ((bf16[16,112,128]{2,1,0:T(8,128)(2,1)}), bf16[16,112,128]{2,1,0:T(8,128)(2,1)S(1)}, u32[]{:S(2)}, u32[]{:S(2)}) async-start(bf16[16,112,128]{2,1,0:T(8,128)(2,1)} %pack.3), calls=%async_computation.2 | async-start | bytes 917504 | tf_op jit(solution)/shard_map/all_to_all | solution.py:576
  35.4 0.0 collective-permute-done.1
  35.4 0.3 collective-permute-done
  35.7 0.0 copy-done.3
  35.7 0.0 copy-done.4
  35.7 0.0 copy-done.5
  35.7 0.0 copy-done.6
  35.8 0.0 copy-done.7
  35.8 9.6 %particles_outer.1 = (f32[3,2,4,1024]{3,2,1,0:T(4,128)S(1)}, bf16[16,128,128]{2,1,0:T(8,128)(2,1)}) custom-call(s32[4,4]{1,0:T(4,128)S(1)} %copy-done.7, bf16[16,112,128]{2,1,0:T(8,128)(2,1)S(1)} %all-to-all-done.recv_ref.refs_1_, f32[3,4,4,1024]{3,2,1,0:T(4,128)S(1)} %copy-done.3, f32[3,4,4,1024]{3,2,1,0:T(4,128)S(1)} %copy-done.4, ...), custom_call_target="tpu_custom_call" | custom-call | flops 8000000000 | bytes 20000000 | tf_op jit(solution)/shard_map/particles_outer/pallas_call | solution.py:379
  45.4 5.6 %all-to-all-done.2.refs_1_ = bf16[16,112,128]{2,1,0:T(8,128)(2,1)S(1)} async-done(((bf16[16,112,128]{2,1,0:T(8,128)(2,1)}), bf16[16,112,128]{2,1,0:T(8,128)(2,1)S(1)}, u32[]{:S(2)}, u32[]{:S(2)}) %all-to-all-start.2) | async-done | bytes 458784 | tf_op jit(solution)/shard_map/all_to_all | solution.py:576
  51.0 3.8 %all-to-all-start.1 = ((bf16[16,128,128]{2,1,0:T(8,128)(2,1)}), bf16[16,128,128]{2,1,0:T(8,128)(2,1)S(1)}, u32[]{:S(2)}, u32[]{:S(2)}) async-start(bf16[16,128,128]{2,1,0:T(8,128)(2,1)} %get-tuple-element.18), calls=%async_computation.1 | async-start | bytes 1048576 | tf_op jit(solution)/shard_map/all_to_all | solution.py:599
  54.8 9.3 %particles_inner.1 = (f32[3,4,4,1024]{3,2,1,0:T(4,128)}, bf16[16,112,128]{2,1,0:T(8,128)(2,1)}) custom-call(s32[4,4]{1,0:T(4,128)S(1)} %copy-done.7, bf16[16,112,128]{2,1,0:T(8,128)(2,1)S(1)} %all-to-all-done.2.refs_1_, f32[3,4,4,1024]{3,2,1,0:T(4,128)S(1)} %copy-done.3, f32[3,4,4,1024]{3,2,1,0:T(4,128)S(1)} %copy-done.4, f32[4,4,1024]{2,1,0:T(4,128)S(1)} %copy-done.5, ...), custom_call_target="tpu_custom_call" | custom-call | flops 8000000000 | bytes 20000000 | tf_op jit(solution)/shard_map/particles_inner/pallas_call | solution.py:379
  64.1 0.0 copy-start
  64.1 6.8 %all-to-all-done.1.recv_ref = bf16[16,128,128]{2,1,0:T(8,128)(2,1)S(1)} async-done(((bf16[16,128,128]{2,1,0:T(8,128)(2,1)}), bf16[16,128,128]{2,1,0:T(8,128)(2,1)S(1)}, u32[]{:S(2)}, u32[]{:S(2)}) %all-to-all-start.1) | async-done | bytes 524320 | tf_op jit(solution)/shard_map/all_to_all | solution.py:599
  70.9 3.6 %all-to-all-start.3 = ((bf16[16,112,128]{2,1,0:T(8,128)(2,1)}), bf16[16,112,128]{2,1,0:T(8,128)(2,1)S(1)}, u32[]{:S(2)}, u32[]{:S(2)}) async-start(bf16[16,112,128]{2,1,0:T(8,128)(2,1)} %get-tuple-element.24), calls=%async_computation.3 | async-start | bytes 917504 | tf_op jit(solution)/shard_map/all_to_all | solution.py:604
  74.5 0.5 gather.2
  75.0 0.1 collective-permute-start.3
  75.1 3.1 %collective-permute-start.2 = (bf16[6,2048]{1,0:T(8,128)(2,1)S(1)}, bf16[6,2048]{1,0:T(8,128)(2,1)S(1)}, u32[]{:S(2)}, u32[]{:S(2)}) collective-permute-start(bf16[6,2048]{1,0:T(8,128)(2,1)S(1)} %get-tuple-element.35), channel_id=1, source_target_pairs={{0,240},{16,32},{32,16},{48,64},{64,48},{80,96},{96,80},{112,128},... | collective-permute-start | bytes 73736 | tf_op jit(solution)/shard_map/ppermute | solution.py:530
  78.2 0.0 collective-permute-done.3
  78.2 6.3 %collective-permute-done.2 = bf16[6,2048]{1,0:T(8,128)(2,1)S(1)} collective-permute-done((bf16[6,2048]{1,0:T(8,128)(2,1)S(1)}, bf16[6,2048]{1,0:T(8,128)(2,1)S(1)}, u32[]{:S(2)}, u32[]{:S(2)}) %collective-permute-start.2) | collective-permute-done | bytes 24608 | tf_op jit(solution)/shard_map/ppermute | solution.py:530
  84.4 5.7 %all-to-all-done.3.recv_ref = bf16[16,112,128]{2,1,0:T(8,128)(2,1)S(1)} async-done(((bf16[16,112,128]{2,1,0:T(8,128)(2,1)}), bf16[16,112,128]{2,1,0:T(8,128)(2,1)S(1)}, u32[]{:S(2)}, u32[]{:S(2)}) %all-to-all-start.3) | async-done | bytes 458784 | tf_op jit(solution)/shard_map/all_to_all | solution.py:604
  90.1 0.0 copy-start.1
  90.1 0.5 gather.3.inner_ref
  90.6 0.0 copy-done
  90.6 0.7 copy-done.1
  91.4 0.0 copy-start.2
  91.4 1.2 %copy-done.2 = bf16[2,4,256,256]{3,2,1,0:T(8,128)(2,1)S(1)} copy-done((bf16[2,4,256,256]{3,2,1,0:T(8,128)(2,1)S(1)}, bf16[2,4,256,256]{3,2,1,0:T(8,128)(2,1)}, u32[]{:S(2)}) %copy-start.2) | copy-done | bytes 1048600
  92.6 5.9 %filter.1 = f32[3072,128]{1,0:T(8,128)} custom-call(f32[3072,128]{1,0:T(8,128)S(1)} %bitcast.12, f32[108,2048]{1,0:T(8,128)S(1)} %get-tuple-element.23.outer_ref, f32[108,2048]{1,0:T(8,128)S(1)} %gather.3.inner_ref, bf16[6,2048]{1,0:T(8,128)(2,1)S(1)} %get-tuple-element.33.from_low_ref, bf16[6,2048]{1,0:T(8,128)(2,1)S(1)} %get-tuple-element.32.from_high_ref, ...), custom_call_target="tpu_custom_call" | custom-call | tf_op jit(solution)/shard_map/filter/pallas_call | solution.py:609
  (4 shorter events, 0.0 us)
Async XLA Ops:
  3.3 23.8 %all-to-all-start = ((bf16[16,112,128]{2,1,0:T(8,128)(2,1)}), bf16[16,112,128]{2,1,0:T(8,128)(2,1)S(1)}, u32[]{:S(2)}, u32[]{:S(2)}) async-start(bf16[16,112,128]{2,1,0:T(8,128)(2,1)} %pack.2), calls=%async_computation | async-start | bytes 917504 | tf_op jit(solution)/shard_map/all_to_all | solution.py:574
  11.9 23.8 %copy-start.3 = (f32[3,4,4,1024]{3,2,1,0:T(4,128)S(1)}, f32[3,4,4,1024]{3,2,1,0:T(4,128)}, u32[]{:S(2)}) copy-start(f32[3,4,4,1024]{3,2,1,0:T(4,128)} %refs_2_.3) | copy-start | bytes 589828
  11.9 23.8 %copy-start.4 = (f32[3,4,4,1024]{3,2,1,0:T(4,128)S(1)}, f32[3,4,4,1024]{3,2,1,0:T(4,128)}, u32[]{:S(2)}) copy-start(f32[3,4,4,1024]{3,2,1,0:T(4,128)} %refs_3_.3) | copy-start | bytes 589828
  11.9 23.8 %copy-start.5 = (f32[4,4,1024]{2,1,0:T(4,128)S(1)}, f32[4,4,1024]{2,1,0:T(4,128)}, u32[]{:S(2)}) copy-start(f32[4,4,1024]{2,1,0:T(4,128)} %refs_4_.3) | copy-start | bytes 196612
  12.0 23.8 %copy-start.6 = (s32[4,4,1024]{2,1,0:T(4,128)S(1)}, s32[4,4,1024]{2,1,0:T(4,128)}, u32[]{:S(2)}) copy-start(s32[4,4,1024]{2,1,0:T(4,128)} %refs_5_.3) | copy-start | bytes 196612
  12.0 23.8 %copy-start.7 = (s32[4,4]{1,0:T(4,128)S(1)}, s32[4,4]{1,0:T(4,128)}, u32[]{:S(2)}) copy-start(s32[4,4]{1,0:T(4,128)} %refs_0_.3) | copy-start | bytes 196
  27.2 8.2 %collective-permute-start.1 = (bf16[160,128]{1,0:T(8,128)(2,1)S(1)}, bf16[160,128]{1,0:T(8,128)(2,1)S(1)}, u32[]{:S(2)}, u32[]{:S(2)}) collective-permute-start(bf16[160,128]{1,0:T(8,128)(2,1)S(1)} %get-tuple-element.30), channel_id=1, source_target_pairs={{0,16},{16,0},{32,48},{48,32},{64,80},{80,64},{96,112},{112,96},{1... | collective-permute-start | bytes 122888 | tf_op jit(solution)/shard_map/ppermute | solution.py:531
  27.3 8.4 %collective-permute-start = (bf16[160,128]{1,0:T(8,128)(2,1)S(1)}, bf16[160,128]{1,0:T(8,128)(2,1)S(1)}, u32[]{:S(2)}, u32[]{:S(2)}) collective-permute-start(bf16[160,128]{1,0:T(8,128)(2,1)S(1)} %get-tuple-element.31), channel_id=1, source_target_pairs={{0,240},{16,32},{32,16},{48,64},{64,48},{80,96},{96,80},{112,128},... | collective-permute-start | bytes 122888 | tf_op jit(solution)/shard_map/ppermute | solution.py:530
  31.8 19.2 %all-to-all-start.2 = ((bf16[16,112,128]{2,1,0:T(8,128)(2,1)}), bf16[16,112,128]{2,1,0:T(8,128)(2,1)S(1)}, u32[]{:S(2)}, u32[]{:S(2)}) async-start(bf16[16,112,128]{2,1,0:T(8,128)(2,1)} %pack.3), calls=%async_computation.2 | async-start | bytes 917504 | tf_op jit(solution)/shard_map/all_to_all | solution.py:576
  51.0 19.9 %all-to-all-start.1 = ((bf16[16,128,128]{2,1,0:T(8,128)(2,1)}), bf16[16,128,128]{2,1,0:T(8,128)(2,1)S(1)}, u32[]{:S(2)}, u32[]{:S(2)}) async-start(bf16[16,128,128]{2,1,0:T(8,128)(2,1)} %get-tuple-element.18), calls=%async_computation.1 | async-start | bytes 1048576 | tf_op jit(solution)/shard_map/all_to_all | solution.py:599
  64.1 26.5 %copy-start = (f32[3,32,2,2048]{3,2,1,0:T(2,128)S(1)}, f32[3,32,2,2048]{3,2,1,0:T(2,128)}, u32[]{:S(2)}) copy-start(f32[3,32,2,2048]{3,2,1,0:T(2,128)} %param.8) | copy-start | bytes 4718596
  70.9 19.2 %all-to-all-start.3 = ((bf16[16,112,128]{2,1,0:T(8,128)(2,1)}), bf16[16,112,128]{2,1,0:T(8,128)(2,1)S(1)}, u32[]{:S(2)}, u32[]{:S(2)}) async-start(bf16[16,112,128]{2,1,0:T(8,128)(2,1)} %get-tuple-element.24), calls=%async_computation.3 | async-start | bytes 917504 | tf_op jit(solution)/shard_map/all_to_all | solution.py:604
  75.0 3.2 %collective-permute-start.3 = (bf16[6,2048]{1,0:T(8,128)(2,1)S(1)}, bf16[6,2048]{1,0:T(8,128)(2,1)S(1)}, u32[]{:S(2)}, u32[]{:S(2)}) collective-permute-start(bf16[6,2048]{1,0:T(8,128)(2,1)S(1)} %get-tuple-element.34), channel_id=1, source_target_pairs={{0,16},{16,0},{32,48},{48,32},{64,80},{80,64},{96,112},{112,96},{1... | collective-permute-start | bytes 73736 | tf_op jit(solution)/shard_map/ppermute | solution.py:531
  75.1 9.4 %collective-permute-start.2 = (bf16[6,2048]{1,0:T(8,128)(2,1)S(1)}, bf16[6,2048]{1,0:T(8,128)(2,1)S(1)}, u32[]{:S(2)}, u32[]{:S(2)}) collective-permute-start(bf16[6,2048]{1,0:T(8,128)(2,1)S(1)} %get-tuple-element.35), channel_id=1, source_target_pairs={{0,240},{16,32},{32,16},{48,64},{64,48},{80,96},{96,80},{112,128},... | collective-permute-start | bytes 73736 | tf_op jit(solution)/shard_map/ppermute | solution.py:530
  90.1 1.2 %copy-start.1 = (bf16[2,4,256,256]{3,2,1,0:T(8,128)(2,1)S(1)}, bf16[2,4,256,256]{3,2,1,0:T(8,128)(2,1)}, u32[]{:S(2)}) copy-start(bf16[2,4,256,256]{3,2,1,0:T(8,128)(2,1)} %constant.26.clone.low_ref) | copy-start | bytes 3145732
  91.4 1.2 %copy-start.2 = (bf16[2,4,256,256]{3,2,1,0:T(8,128)(2,1)S(1)}, bf16[2,4,256,256]{3,2,1,0:T(8,128)(2,1)}, u32[]{:S(2)}) copy-start(bf16[2,4,256,256]{3,2,1,0:T(8,128)(2,1)} %constant.25.clone.high_ref) | copy-start | bytes 3145732

commit v2 on v1

--- a/solution.py
+++ b/solution.py
@@ -459,7 +459,7 @@
 
 def filter_kernel(
     dims, outer_pieces, inner_piece, grid_ref, outer_ref, inner_ref, from_low_ref, from_high_ref,
-    high_ref, low_ref, out_ref, mixed, dep,
+    taps_ref, out_ref, mixed, dep,
 ):
     width, devices, planes = dims
     depth = devices * planes
@@ -480,8 +480,8 @@
                 lanes = slice(j * LANES, (j + 1) * LANES)
                 fluid = grid_ref[pl.ds(c * width * depth + j * planes + p, width, stride=depth), :]
                 mixed[pl.ds(e * width, width), lanes] = fluid + dep[0:width, lanes].astype(bf16).astype(f32)
-    folds = high_ref.shape[1]
-    block = high_ref.shape[2]
+    folds = taps_ref.shape[2]
+    block = taps_ref.shape[3]
     sides = []
     for sign in range(2):
         highs, lows = [], []
@@ -501,9 +501,9 @@
             for i in range(folds):
                 d = (o - i) % folds
                 key = -1 if sign == 1 and o < i else 1
-                part = jnp.dot(highs[i], high_ref[sign, d], preferred_element_type=f32)
-                part = part + jnp.dot(lows[i], high_ref[sign, d], preferred_element_type=f32)
-                part = part + jnp.dot(highs[i], low_ref[sign, d], preferred_element_type=f32)
+                part = jnp.dot(highs[i], taps_ref[0, sign, d], preferred_element_type=f32)
+                part = part + jnp.dot(lows[i], taps_ref[0, sign, d], preferred_element_type=f32)
+                part = part + jnp.dot(highs[i], taps_ref[1, sign, d], preferred_element_type=f32)
                 sums[key] = part if sums[key] is None else sums[key] + part
             results.append(sums[1] if sums[-1] is None else sums[1] - sums[-1])
         for flip in range(2):
@@ -609,7 +609,7 @@
     out = pl.pallas_call(
         functools.partial(filter_kernel, dims, outer, inner),
         out_shape=jax.ShapeDtypeStruct(grid.shape, f32),
-        in_specs=[vmem] * 7,
+        in_specs=[vmem] * 6,
         out_specs=vmem,
         scratch_shapes=[
             pltpu.VMEM((planes * COMPS * width, length), f32),
@@ -617,7 +617,7 @@
         ],
         compiler_params=params,
         name="filter",
-    )(grid, dep_outer, dep_inner, from_low, from_high, jnp.asarray(taps_high), jnp.asarray(taps_low))
+    )(grid, dep_outer, dep_inner, from_low, from_high, jnp.asarray(np.stack([taps_high, taps_low])))
     out = out.reshape(COMPS * width, devices, planes, LANES).transpose(0, 2, 1, 3)
     return out.reshape(fluid.shape), vel_next
 

time: 99.1 us -> 98.7 us (level)
    unnamed x16 -> x14, local copies, waits for them, and re-layouts: 1.98 us -> 1.62 us
  transfers between devices with their start and end apart: 8 -> 8, of which waited for: 6 -> 6; matrix products, arithmetic and copies ran while one was open for 0% -> 0% of each run, Pallas kernels for 22% -> 23%
where the time goes in v2:
time: 98.7 us; the launch traced here: 98.1 us
  waiting for transfers between devices  37 us (37%)
  Pallas kernels  31.2 us (32%)
  starting transfers between devices  27.4 us (28%)
  local copies, waits for them, and re-layouts  1.62 us (2%)
    pallas_call x2, Pallas kernels, particle_call(): pl.pallas_call(functools.partial(particle_kernel, dims, plan), out_shape=...  19 us
    all_to_all x1, waiting for transfers between devices, per_device(): recv_outer = lax.all_to_all(send_outer, 'py', 0, 0, tiled=True)  12.3 us
    all_to_all x1, starting transfers between devices, per_device(): recv_outer = lax.all_to_all(send_outer, 'py', 0, 0, tiled=True)  8.65 us
    ppermute x2, starting transfers between devices, exchange(): far = lax.ppermute(jnp.where(even, low, high), 'px', second)  7.64 us
    all_to_all x1, waiting for transfers between devices, per_device(): pencil_outer = lax.all_to_all(back_outer, 'py', 0, 0, tiled=True)  6.77 us
    ppermute x2, waiting for transfers between devices, exchange(): far = lax.ppermute(jnp.where(even, low, high), 'px', second)  6.55 us
    pallas_call x1, Pallas kernels, per_device(): pl.pallas_call(functools.partial(filter_kernel, dims, outer, inner), out_...  5.86 us
    all_to_all x1, waiting for transfers between devices, per_device(): pencil_inner = lax.all_to_all(back_inner, 'py', 0, 0, tiled=True)  5.69 us
  transfers between devices with their start and end apart: 8, of which 6 were waited for; matrix products, arithmetic and copies ran while one was open for 0% of the time, Pallas kernels for 23%

profile of v2, /device:TPU:2, one launch (start us, length us, event | category | flops | bytes accessed | tf_op | source)
XLA Modules:
  0.0 98.1 jit_solution(3338038178022057263)
XLA Ops:
  0.6 2.6 %pack.2 = bf16[16,112,128]{2,1,0:T(8,128)(2,1)} custom-call(f32[3072,128]{1,0:T(8,128)} %bitcast.10), custom_call_target="tpu_custom_call" | custom-call | flops 100000000 | bytes 2000000 | tf_op jit(solution)/shard_map/pack/pallas_call | solution.py:557
  3.3 8.6 %all-to-all-start = ((bf16[16,112,128]{2,1,0:T(8,128)(2,1)}), bf16[16,112,128]{2,1,0:T(8,128)(2,1)S(1)}, u32[]{:S(2)}, u32[]{:S(2)}) async-start(bf16[16,112,128]{2,1,0:T(8,128)(2,1)} %pack.2), calls=%async_computation | async-start | bytes 917504 | tf_op jit(solution)/shard_map/all_to_all | solution.py:574
  11.9 0.0 copy-start.2
  11.9 0.0 copy-start.3
  11.9 0.0 copy-start.4
  12.0 0.0 copy-start.5
  12.0 0.0 copy-start.6
  12.0 2.7 %pack.3 = bf16[16,112,128]{2,1,0:T(8,128)(2,1)} custom-call(f32[3072,128]{1,0:T(8,128)} %bitcast.11), custom_call_target="tpu_custom_call" | custom-call | flops 100000000 | bytes 2000000 | tf_op jit(solution)/shard_map/pack/pallas_call | solution.py:557
  14.7 12.3 %all-to-all-done.recv_ref.refs_1_ = bf16[16,112,128]{2,1,0:T(8,128)(2,1)S(1)} async-done(((bf16[16,112,128]{2,1,0:T(8,128)(2,1)}), bf16[16,112,128]{2,1,0:T(8,128)(2,1)S(1)}, u32[]{:S(2)}, u32[]{:S(2)}) %all-to-all-start) | async-done | bytes 458784 | tf_op jit(solution)/shard_map/all_to_all | solution.py:574
  27.0 0.1 edges.1
  27.2 0.1 collective-permute-start.1
  27.3 4.6 %collective-permute-start = (bf16[160,128]{1,0:T(8,128)(2,1)S(1)}, bf16[160,128]{1,0:T(8,128)(2,1)S(1)}, u32[]{:S(2)}, u32[]{:S(2)}) collective-permute-start(bf16[160,128]{1,0:T(8,128)(2,1)S(1)} %get-tuple-element.31), channel_id=1, source_target_pairs={{0,240},{16,32},{32,16},{48,64},{64,48},{80,96},{96,80},{112,128},... | collective-permute-start | bytes 122888 | tf_op jit(solution)/shard_map/ppermute | solution.py:530
  31.8 3.6 %all-to-all-start.2 = ((bf16[16,112,128]{2,1,0:T(8,128)(2,1)}), bf16[16,112,128]{2,1,0:T(8,128)(2,1)S(1)}, u32[]{:S(2)}, u32[]{:S(2)}) async-start(bf16[16,112,128]{2,1,0:T(8,128)(2,1)} %pack.3), calls=%async_computation.2 | async-start | bytes 917504 | tf_op jit(solution)/shard_map/all_to_all | solution.py:576
  35.4 0.0 collective-permute-done.1
  35.4 0.3 collective-permute-done
  35.7 0.0 copy-done.2
  35.7 0.0 copy-done.3
  35.7 0.0 copy-done.4
  35.7 0.0 copy-done.5
  35.8 0.0 copy-done.6
  35.8 9.6 %particles_outer.1 = (f32[3,2,4,1024]{3,2,1,0:T(4,128)S(1)}, bf16[16,128,128]{2,1,0:T(8,128)(2,1)}) custom-call(s32[4,4]{1,0:T(4,128)S(1)} %copy-done.6, bf16[16,112,128]{2,1,0:T(8,128)(2,1)S(1)} %all-to-all-done.recv_ref.refs_1_, f32[3,4,4,1024]{3,2,1,0:T(4,128)S(1)} %copy-done.2, f32[3,4,4,1024]{3,2,1,0:T(4,128)S(1)} %copy-done.3, ...), custom_call_target="tpu_custom_call" | custom-call | flops 8000000000 | bytes 20000000 | tf_op jit(solution)/shard_map/particles_outer/pallas_call | solution.py:379
  45.4 5.6 %all-to-all-done.2.refs_1_ = bf16[16,112,128]{2,1,0:T(8,128)(2,1)S(1)} async-done(((bf16[16,112,128]{2,1,0:T(8,128)(2,1)}), bf16[16,112,128]{2,1,0:T(8,128)(2,1)S(1)}, u32[]{:S(2)}, u32[]{:S(2)}) %all-to-all-start.2) | async-done | bytes 458784 | tf_op jit(solution)/shard_map/all_to_all | solution.py:576
  51.0 3.8 %all-to-all-start.1 = ((bf16[16,128,128]{2,1,0:T(8,128)(2,1)}), bf16[16,128,128]{2,1,0:T(8,128)(2,1)S(1)}, u32[]{:S(2)}, u32[]{:S(2)}) async-start(bf16[16,128,128]{2,1,0:T(8,128)(2,1)} %get-tuple-element.18), calls=%async_computation.1 | async-start | bytes 1048576 | tf_op jit(solution)/shard_map/all_to_all | solution.py:599
  54.8 9.3 %particles_inner.1 = (f32[3,4,4,1024]{3,2,1,0:T(4,128)}, bf16[16,112,128]{2,1,0:T(8,128)(2,1)}) custom-call(s32[4,4]{1,0:T(4,128)S(1)} %copy-done.6, bf16[16,112,128]{2,1,0:T(8,128)(2,1)S(1)} %all-to-all-done.2.refs_1_, f32[3,4,4,1024]{3,2,1,0:T(4,128)S(1)} %copy-done.2, f32[3,4,4,1024]{3,2,1,0:T(4,128)S(1)} %copy-done.3, f32[4,4,1024]{2,1,0:T(4,128)S(1)} %copy-done.4, ...), custom_call_target="tpu_custom_call" | custom-call | flops 8000000000 | bytes 20000000 | tf_op jit(solution)/shard_map/particles_inner/pallas_call | solution.py:379
  64.1 0.0 copy-start
  64.1 6.8 %all-to-all-done.1.recv_ref = bf16[16,128,128]{2,1,0:T(8,128)(2,1)S(1)} async-done(((bf16[16,128,128]{2,1,0:T(8,128)(2,1)}), bf16[16,128,128]{2,1,0:T(8,128)(2,1)S(1)}, u32[]{:S(2)}, u32[]{:S(2)}) %all-to-all-start.1) | async-done | bytes 524320 | tf_op jit(solution)/shard_map/all_to_all | solution.py:599
  70.9 3.6 %all-to-all-start.3 = ((bf16[16,112,128]{2,1,0:T(8,128)(2,1)}), bf16[16,112,128]{2,1,0:T(8,128)(2,1)S(1)}, u32[]{:S(2)}, u32[]{:S(2)}) async-start(bf16[16,112,128]{2,1,0:T(8,128)(2,1)} %get-tuple-element.24), calls=%async_computation.3 | async-start | bytes 917504 | tf_op jit(solution)/shard_map/all_to_all | solution.py:604
  74.5 0.5 gather.2
  75.0 0.1 collective-permute-start.3
  75.1 3.1 %collective-permute-start.2 = (bf16[6,2048]{1,0:T(8,128)(2,1)S(1)}, bf16[6,2048]{1,0:T(8,128)(2,1)S(1)}, u32[]{:S(2)}, u32[]{:S(2)}) collective-permute-start(bf16[6,2048]{1,0:T(8,128)(2,1)S(1)} %get-tuple-element.35), channel_id=1, source_target_pairs={{0,240},{16,32},{32,16},{48,64},{64,48},{80,96},{96,80},{112,128},... | collective-permute-start | bytes 73736 | tf_op jit(solution)/shard_map/ppermute | solution.py:530
  78.2 0.0 collective-permute-done.3
  78.2 6.3 %collective-permute-done.2 = bf16[6,2048]{1,0:T(8,128)(2,1)S(1)} collective-permute-done((bf16[6,2048]{1,0:T(8,128)(2,1)S(1)}, bf16[6,2048]{1,0:T(8,128)(2,1)S(1)}, u32[]{:S(2)}, u32[]{:S(2)}) %collective-permute-start.2) | collective-permute-done | bytes 24608 | tf_op jit(solution)/shard_map/ppermute | solution.py:530
  84.4 5.7 %all-to-all-done.3.recv_ref = bf16[16,112,128]{2,1,0:T(8,128)(2,1)S(1)} async-done(((bf16[16,112,128]{2,1,0:T(8,128)(2,1)}), bf16[16,112,128]{2,1,0:T(8,128)(2,1)S(1)}, u32[]{:S(2)}, u32[]{:S(2)}) %all-to-all-start.3) | async-done | bytes 458784 | tf_op jit(solution)/shard_map/all_to_all | solution.py:604
  90.1 0.5 gather.3.inner_ref
  90.6 0.0 copy-done
  90.6 0.0 copy-start.1
  90.6 1.6 %copy-done.1 = bf16[2,2,4,256,256]{4,3,2,1,0:T(8,128)(2,1)S(1)} copy-done((bf16[2,2,4,256,256]{4,3,2,1,0:T(8,128)(2,1)S(1)}, bf16[2,2,4,256,256]{4,3,2,1,0:T(8,128)(2,1)}, u32[]{:S(2)}) %copy-start.1) | copy-done | bytes 2097176
  92.2 5.9 %filter.1 = f32[3072,128]{1,0:T(8,128)} custom-call(f32[3072,128]{1,0:T(8,128)S(1)} %bitcast.12, f32[108,2048]{1,0:T(8,128)S(1)} %get-tuple-element.23.outer_ref, f32[108,2048]{1,0:T(8,128)S(1)} %gather.3.inner_ref, bf16[6,2048]{1,0:T(8,128)(2,1)S(1)} %get-tuple-element.33.from_low_ref, bf16[6,2048]{1,0:T(8,128)(2,1)S(1)} %get-tuple-element.32.from_high_ref, ...), custom_call_target="tpu_custom_call" | custom-call | tf_op jit(solution)/shard_map/filter/pallas_call | solution.py:609
  (4 shorter events, 0.0 us)
Async XLA Ops:
  3.3 23.8 %all-to-all-start = ((bf16[16,112,128]{2,1,0:T(8,128)(2,1)}), bf16[16,112,128]{2,1,0:T(8,128)(2,1)S(1)}, u32[]{:S(2)}, u32[]{:S(2)}) async-start(bf16[16,112,128]{2,1,0:T(8,128)(2,1)} %pack.2), calls=%async_computation | async-start | bytes 917504 | tf_op jit(solution)/shard_map/all_to_all | solution.py:574
  11.9 23.8 %copy-start.2 = (f32[3,4,4,1024]{3,2,1,0:T(4,128)S(1)}, f32[3,4,4,1024]{3,2,1,0:T(4,128)}, u32[]{:S(2)}) copy-start(f32[3,4,4,1024]{3,2,1,0:T(4,128)} %refs_2_.3) | copy-start | bytes 589828
  11.9 23.8 %copy-start.3 = (f32[3,4,4,1024]{3,2,1,0:T(4,128)S(1)}, f32[3,4,4,1024]{3,2,1,0:T(4,128)}, u32[]{:S(2)}) copy-start(f32[3,4,4,1024]{3,2,1,0:T(4,128)} %refs_3_.3) | copy-start | bytes 589828
  11.9 23.8 %copy-start.4 = (f32[4,4,1024]{2,1,0:T(4,128)S(1)}, f32[4,4,1024]{2,1,0:T(4,128)}, u32[]{:S(2)}) copy-start(f32[4,4,1024]{2,1,0:T(4,128)} %refs_4_.3) | copy-start | bytes 196612
  12.0 23.8 %copy-start.5 = (s32[4,4,1024]{2,1,0:T(4,128)S(1)}, s32[4,4,1024]{2,1,0:T(4,128)}, u32[]{:S(2)}) copy-start(s32[4,4,1024]{2,1,0:T(4,128)} %refs_5_.3) | copy-start | bytes 196612
  12.0 23.8 %copy-start.6 = (s32[4,4]{1,0:T(4,128)S(1)}, s32[4,4]{1,0:T(4,128)}, u32[]{:S(2)}) copy-start(s32[4,4]{1,0:T(4,128)} %refs_0_.3) | copy-start | bytes 196
  27.2 8.2 %collective-permute-start.1 = (bf16[160,128]{1,0:T(8,128)(2,1)S(1)}, bf16[160,128]{1,0:T(8,128)(2,1)S(1)}, u32[]{:S(2)}, u32[]{:S(2)}) collective-permute-start(bf16[160,128]{1,0:T(8,128)(2,1)S(1)} %get-tuple-element.30), channel_id=1, source_target_pairs={{0,16},{16,0},{32,48},{48,32},{64,80},{80,64},{96,112},{112,96},{1... | collective-permute-start | bytes 122888 | tf_op jit(solution)/shard_map/ppermute | solution.py:531
  27.3 8.4 %collective-permute-start = (bf16[160,128]{1,0:T(8,128)(2,1)S(1)}, bf16[160,128]{1,0:T(8,128)(2,1)S(1)}, u32[]{:S(2)}, u32[]{:S(2)}) collective-permute-start(bf16[160,128]{1,0:T(8,128)(2,1)S(1)} %get-tuple-element.31), channel_id=1, source_target_pairs={{0,240},{16,32},{32,16},{48,64},{64,48},{80,96},{96,80},{112,128},... | collective-permute-start | bytes 122888 | tf_op jit(solution)/shard_map/ppermute | solution.py:530
  31.8 19.2 %all-to-all-start.2 = ((bf16[16,112,128]{2,1,0:T(8,128)(2,1)}), bf16[16,112,128]{2,1,0:T(8,128)(2,1)S(1)}, u32[]{:S(2)}, u32[]{:S(2)}) async-start(bf16[16,112,128]{2,1,0:T(8,128)(2,1)} %pack.3), calls=%async_computation.2 | async-start | bytes 917504 | tf_op jit(solution)/shard_map/all_to_all | solution.py:576
  51.0 19.9 %all-to-all-start.1 = ((bf16[16,128,128]{2,1,0:T(8,128)(2,1)}), bf16[16,128,128]{2,1,0:T(8,128)(2,1)S(1)}, u32[]{:S(2)}, u32[]{:S(2)}) async-start(bf16[16,128,128]{2,1,0:T(8,128)(2,1)} %get-tuple-element.18), calls=%async_computation.1 | async-start | bytes 1048576 | tf_op jit(solution)/shard_map/all_to_all | solution.py:599
  64.1 26.5 %copy-start = (f32[3,32,2,2048]{3,2,1,0:T(2,128)S(1)}, f32[3,32,2,2048]{3,2,1,0:T(2,128)}, u32[]{:S(2)}) copy-start(f32[3,32,2,2048]{3,2,1,0:T(2,128)} %param.7) | copy-start | bytes 4718596
  70.9 19.2 %all-to-all-start.3 = ((bf16[16,112,128]{2,1,0:T(8,128)(2,1)}), bf16[16,112,128]{2,1,0:T(8,128)(2,1)S(1)}, u32[]{:S(2)}, u32[]{:S(2)}) async-start(bf16[16,112,128]{2,1,0:T(8,128)(2,1)} %get-tuple-element.24), calls=%async_computation.3 | async-start | bytes 917504 | tf_op jit(solution)/shard_map/all_to_all | solution.py:604
  75.0 3.2 %collective-permute-start.3 = (bf16[6,2048]{1,0:T(8,128)(2,1)S(1)}, bf16[6,2048]{1,0:T(8,128)(2,1)S(1)}, u32[]{:S(2)}, u32[]{:S(2)}) collective-permute-start(bf16[6,2048]{1,0:T(8,128)(2,1)S(1)} %get-tuple-element.34), channel_id=1, source_target_pairs={{0,16},{16,0},{32,48},{48,32},{64,80},{80,64},{96,112},{112,96},{1... | collective-permute-start | bytes 73736 | tf_op jit(solution)/shard_map/ppermute | solution.py:531
  75.1 9.4 %collective-permute-start.2 = (bf16[6,2048]{1,0:T(8,128)(2,1)S(1)}, bf16[6,2048]{1,0:T(8,128)(2,1)S(1)}, u32[]{:S(2)}, u32[]{:S(2)}) collective-permute-start(bf16[6,2048]{1,0:T(8,128)(2,1)S(1)} %get-tuple-element.35), channel_id=1, source_target_pairs={{0,240},{16,32},{32,16},{48,64},{64,48},{80,96},{96,80},{112,128},... | collective-permute-start | bytes 73736 | tf_op jit(solution)/shard_map/ppermute | solution.py:530
  90.6 1.6 %copy-start.1 = (bf16[2,2,4,256,256]{4,3,2,1,0:T(8,128)(2,1)S(1)}, bf16[2,2,4,256,256]{4,3,2,1,0:T(8,128)(2,1)}, u32[]{:S(2)}) copy-start(bf16[2,2,4,256,256]{4,3,2,1,0:T(8,128)(2,1)} %constant.23.clone.taps_ref) | copy-start | bytes 6291460

commit v3 on v2

--- a/solution.py
+++ b/solution.py
@@ -22,6 +22,7 @@
 f32 = jnp.float32
 bf16 = jnp.bfloat16
 NT = (((1,), (1,)), ((), ()))
+NN = (((1,), (0,)), ((), ()))
 
 
 def filter_blocks(length, width):
@@ -480,8 +481,8 @@
                 lanes = slice(j * LANES, (j + 1) * LANES)
                 fluid = grid_ref[pl.ds(c * width * depth + j * planes + p, width, stride=depth), :]
                 mixed[pl.ds(e * width, width), lanes] = fluid + dep[0:width, lanes].astype(bf16).astype(f32)
-    folds = taps_ref.shape[2]
     block = taps_ref.shape[3]
+    folds = mixed.shape[1] // block // 2
     sides = []
     for sign in range(2):
         highs, lows = [], []
@@ -501,9 +502,14 @@
             for i in range(folds):
                 d = (o - i) % folds
                 key = -1 if sign == 1 and o < i else 1
-                part = jnp.dot(highs[i], taps_ref[0, sign, d], preferred_element_type=f32)
-                part = part + jnp.dot(lows[i], taps_ref[0, sign, d], preferred_element_type=f32)
-                part = part + jnp.dot(highs[i], taps_ref[1, sign, d], preferred_element_type=f32)
+                kind = NN
+                if d > folds // 2:
+                    d, kind = folds - d, NT
+                    key = -key if sign == 1 else key
+                high, low = taps_ref[0, sign, d], taps_ref[1, sign, d]
+                part = lax.dot_general(highs[i], high, kind, preferred_element_type=f32)
+                part = part + lax.dot_general(lows[i], high, kind, preferred_element_type=f32)
+                part = part + lax.dot_general(highs[i], low, kind, preferred_element_type=f32)
                 sums[key] = part if sums[key] is None else sums[key] + part
             results.append(sums[1] if sums[-1] is None else sums[1] - sums[-1])
         for flip in range(2):
@@ -617,7 +623,7 @@
         ],
         compiler_params=params,
         name="filter",
-    )(grid, dep_outer, dep_inner, from_low, from_high, jnp.asarray(np.stack([taps_high, taps_low])))
+    )(grid, dep_outer, dep_inner, from_low, from_high, jnp.asarray(np.stack([taps_high, taps_low])[:, :, : length // 1024 + 1]))
     out = out.reshape(COMPS * width, devices, planes, LANES).transpose(0, 2, 1, 3)
     return out.reshape(fluid.shape), vel_next
 

time: 98.7 us -> 98.8 us (level)
  no operation moved by 1% of the time
where the time goes in v3:
time: 98.8 us; the launch traced here: 98.2 us
  waiting for transfers between devices  37 us (37%)
  Pallas kernels  31.5 us (32%)
  starting transfers between devices  27.4 us (28%)
  local copies, waits for them, and re-layouts  1.44 us (1%)
    pallas_call x2, Pallas kernels, particle_call(): pl.pallas_call(functools.partial(particle_kernel, dims, plan), out_shape=...  19 us
    all_to_all x1, waiting for transfers between devices, per_device(): recv_outer = lax.all_to_all(send_outer, 'py', 0, 0, tiled=True)  12.3 us
    all_to_all x1, starting transfers between devices, per_device(): recv_outer = lax.all_to_all(send_outer, 'py', 0, 0, tiled=True)  8.65 us
    ppermute x2, starting transfers between devices, exchange(): far = lax.ppermute(jnp.where(even, low, high), 'px', second)  7.64 us
    all_to_all x1, waiting for transfers between devices, per_device(): pencil_outer = lax.all_to_all(back_outer, 'py', 0, 0, tiled=True)  6.77 us
    ppermute x2, waiting for transfers between devices, exchange(): far = lax.ppermute(jnp.where(even, low, high), 'px', second)  6.55 us
    pallas_call x1, Pallas kernels, per_device(): pl.pallas_call(functools.partial(filter_kernel, dims, outer, inner), out_...  6.14 us
    all_to_all x1, waiting for transfers between devices, per_device(): pencil_inner = lax.all_to_all(back_inner, 'py', 0, 0, tiled=True)  5.69 us
  transfers between devices with their start and end apart: 8, of which 6 were waited for; matrix products, arithmetic and copies ran while one was open for 0% of the time, Pallas kernels for 23%

profile of v3, /device:TPU:2, one launch (start us, length us, event | category | flops | bytes accessed | tf_op | source)
XLA Modules:
  0.0 98.2 jit_solution(1263759483039952679)
XLA Ops:
  0.6 2.6 %pack.2 = bf16[16,112,128]{2,1,0:T(8,128)(2,1)} custom-call(f32[3072,128]{1,0:T(8,128)} %bitcast.10), custom_call_target="tpu_custom_call" | custom-call | flops 100000000 | bytes 2000000 | tf_op jit(solution)/shard_map/pack/pallas_call | solution.py:563
  3.3 8.6 %all-to-all-start = ((bf16[16,112,128]{2,1,0:T(8,128)(2,1)}), bf16[16,112,128]{2,1,0:T(8,128)(2,1)S(1)}, u32[]{:S(2)}, u32[]{:S(2)}) async-start(bf16[16,112,128]{2,1,0:T(8,128)(2,1)} %pack.2), calls=%async_computation | async-start | bytes 917504 | tf_op jit(solution)/shard_map/all_to_all | solution.py:580
  11.9 0.0 copy-start.2
  11.9 0.0 copy-start.3
  11.9 0.0 copy-start.4
  12.0 0.0 copy-start.5
  12.0 0.0 copy-start.6
  12.0 2.7 %pack.3 = bf16[16,112,128]{2,1,0:T(8,128)(2,1)} custom-call(f32[3072,128]{1,0:T(8,128)} %bitcast.11), custom_call_target="tpu_custom_call" | custom-call | flops 100000000 | bytes 2000000 | tf_op jit(solution)/shard_map/pack/pallas_call | solution.py:563
  14.7 12.3 %all-to-all-done.recv_ref.refs_1_ = bf16[16,112,128]{2,1,0:T(8,128)(2,1)S(1)} async-done(((bf16[16,112,128]{2,1,0:T(8,128)(2,1)}), bf16[16,112,128]{2,1,0:T(8,128)(2,1)S(1)}, u32[]{:S(2)}, u32[]{:S(2)}) %all-to-all-start) | async-done | bytes 458784 | tf_op jit(solution)/shard_map/all_to_all | solution.py:580
  27.0 0.1 edges.1
  27.2 0.1 collective-permute-start.1
  27.3 4.6 %collective-permute-start = (bf16[160,128]{1,0:T(8,128)(2,1)S(1)}, bf16[160,128]{1,0:T(8,128)(2,1)S(1)}, u32[]{:S(2)}, u32[]{:S(2)}) collective-permute-start(bf16[160,128]{1,0:T(8,128)(2,1)S(1)} %get-tuple-element.31), channel_id=1, source_target_pairs={{0,240},{16,32},{32,16},{48,64},{64,48},{80,96},{96,80},{112,128},... | collective-permute-start | bytes 122888 | tf_op jit(solution)/shard_map/ppermute | solution.py:536
  31.8 3.6 %all-to-all-start.2 = ((bf16[16,112,128]{2,1,0:T(8,128)(2,1)}), bf16[16,112,128]{2,1,0:T(8,128)(2,1)S(1)}, u32[]{:S(2)}, u32[]{:S(2)}) async-start(bf16[16,112,128]{2,1,0:T(8,128)(2,1)} %pack.3), calls=%async_computation.2 | async-start | bytes 917504 | tf_op jit(solution)/shard_map/all_to_all | solution.py:582
  35.4 0.0 collective-permute-done.1
  35.4 0.3 collective-permute-done
  35.7 0.0 copy-done.2
  35.7 0.0 copy-done.3
  35.7 0.0 copy-done.4
  35.7 0.0 copy-done.5
  35.8 0.0 copy-done.6
  35.8 9.6 %particles_outer.1 = (f32[3,2,4,1024]{3,2,1,0:T(4,128)S(1)}, bf16[16,128,128]{2,1,0:T(8,128)(2,1)}) custom-call(s32[4,4]{1,0:T(4,128)S(1)} %copy-done.6, bf16[16,112,128]{2,1,0:T(8,128)(2,1)S(1)} %all-to-all-done.recv_ref.refs_1_, f32[3,4,4,1024]{3,2,1,0:T(4,128)S(1)} %copy-done.2, f32[3,4,4,1024]{3,2,1,0:T(4,128)S(1)} %copy-done.3, ...), custom_call_target="tpu_custom_call" | custom-call | flops 8000000000 | bytes 20000000 | tf_op jit(solution)/shard_map/particles_outer/pallas_call | solution.py:380
  45.4 5.6 %all-to-all-done.2.refs_1_ = bf16[16,112,128]{2,1,0:T(8,128)(2,1)S(1)} async-done(((bf16[16,112,128]{2,1,0:T(8,128)(2,1)}), bf16[16,112,128]{2,1,0:T(8,128)(2,1)S(1)}, u32[]{:S(2)}, u32[]{:S(2)}) %all-to-all-start.2) | async-done | bytes 458784 | tf_op jit(solution)/shard_map/all_to_all | solution.py:582
  51.0 3.8 %all-to-all-start.1 = ((bf16[16,128,128]{2,1,0:T(8,128)(2,1)}), bf16[16,128,128]{2,1,0:T(8,128)(2,1)S(1)}, u32[]{:S(2)}, u32[]{:S(2)}) async-start(bf16[16,128,128]{2,1,0:T(8,128)(2,1)} %get-tuple-element.18), calls=%async_computation.1 | async-start | bytes 1048576 | tf_op jit(solution)/shard_map/all_to_all | solution.py:605
  54.8 9.3 %particles_inner.1 = (f32[3,4,4,1024]{3,2,1,0:T(4,128)}, bf16[16,112,128]{2,1,0:T(8,128)(2,1)}) custom-call(s32[4,4]{1,0:T(4,128)S(1)} %copy-done.6, bf16[16,112,128]{2,1,0:T(8,128)(2,1)S(1)} %all-to-all-done.2.refs_1_, f32[3,4,4,1024]{3,2,1,0:T(4,128)S(1)} %copy-done.2, f32[3,4,4,1024]{3,2,1,0:T(4,128)S(1)} %copy-done.3, f32[4,4,1024]{2,1,0:T(4,128)S(1)} %copy-done.4, ...), custom_call_target="tpu_custom_call" | custom-call | flops 8000000000 | bytes 20000000 | tf_op jit(solution)/shard_map/particles_inner/pallas_call | solution.py:380
  64.1 0.0 copy-start
  64.1 6.8 %all-to-all-done.1.recv_ref = bf16[16,128,128]{2,1,0:T(8,128)(2,1)S(1)} async-done(((bf16[16,128,128]{2,1,0:T(8,128)(2,1)}), bf16[16,128,128]{2,1,0:T(8,128)(2,1)S(1)}, u32[]{:S(2)}, u32[]{:S(2)}) %all-to-all-start.1) | async-done | bytes 524320 | tf_op jit(solution)/shard_map/all_to_all | solution.py:605
  70.9 3.6 %all-to-all-start.3 = ((bf16[16,112,128]{2,1,0:T(8,128)(2,1)}), bf16[16,112,128]{2,1,0:T(8,128)(2,1)S(1)}, u32[]{:S(2)}, u32[]{:S(2)}) async-start(bf16[16,112,128]{2,1,0:T(8,128)(2,1)} %get-tuple-element.24), calls=%async_computation.3 | async-start | bytes 917504 | tf_op jit(solution)/shard_map/all_to_all | solution.py:610
  74.5 0.5 gather.2
  75.0 0.1 collective-permute-start.3
  75.1 3.1 %collective-permute-start.2 = (bf16[6,2048]{1,0:T(8,128)(2,1)S(1)}, bf16[6,2048]{1,0:T(8,128)(2,1)S(1)}, u32[]{:S(2)}, u32[]{:S(2)}) collective-permute-start(bf16[6,2048]{1,0:T(8,128)(2,1)S(1)} %get-tuple-element.35), channel_id=1, source_target_pairs={{0,240},{16,32},{32,16},{48,64},{64,48},{80,96},{96,80},{112,128},... | collective-permute-start | bytes 73736 | tf_op jit(solution)/shard_map/ppermute | solution.py:536
  78.2 0.0 collective-permute-done.3
  78.2 6.3 %collective-permute-done.2 = bf16[6,2048]{1,0:T(8,128)(2,1)S(1)} collective-permute-done((bf16[6,2048]{1,0:T(8,128)(2,1)S(1)}, bf16[6,2048]{1,0:T(8,128)(2,1)S(1)}, u32[]{:S(2)}, u32[]{:S(2)}) %collective-permute-start.2) | collective-permute-done | bytes 24608 | tf_op jit(solution)/shard_map/ppermute | solution.py:536
  84.4 5.7 %all-to-all-done.3.recv_ref = bf16[16,112,128]{2,1,0:T(8,128)(2,1)S(1)} async-done(((bf16[16,112,128]{2,1,0:T(8,128)(2,1)}), bf16[16,112,128]{2,1,0:T(8,128)(2,1)S(1)}, u32[]{:S(2)}, u32[]{:S(2)}) %all-to-all-start.3) | async-done | bytes 458784 | tf_op jit(solution)/shard_map/all_to_all | solution.py:610
  90.1 0.5 gather.3.inner_ref
  90.6 0.0 copy-done
  90.6 0.0 copy-start.1
  90.6 1.4 %copy-done.1 = bf16[2,2,3,256,256]{4,3,2,1,0:T(8,128)(2,1)S(1)} copy-done((bf16[2,2,3,256,256]{4,3,2,1,0:T(8,128)(2,1)S(1)}, bf16[2,2,3,256,256]{4,3,2,1,0:T(8,128)(2,1)}, u32[]{:S(2)}) %copy-start.1) | copy-done | bytes 1572888
  92.0 6.1 %filter.1 = f32[3072,128]{1,0:T(8,128)} custom-call(f32[3072,128]{1,0:T(8,128)S(1)} %bitcast.12, f32[108,2048]{1,0:T(8,128)S(1)} %get-tuple-element.23.outer_ref, f32[108,2048]{1,0:T(8,128)S(1)} %gather.3.inner_ref, bf16[6,2048]{1,0:T(8,128)(2,1)S(1)} %get-tuple-element.33.from_low_ref, bf16[6,2048]{1,0:T(8,128)(2,1)S(1)} %get-tuple-element.32.from_high_ref, ...), custom_call_target="tpu_custom_call" | custom-call | tf_op jit(solution)/shard_map/filter/pallas_call | solution.py:615
  (4 shorter events, 0.0 us)
Async XLA Ops:
  3.3 23.8 %all-to-all-start = ((bf16[16,112,128]{2,1,0:T(8,128)(2,1)}), bf16[16,112,128]{2,1,0:T(8,128)(2,1)S(1)}, u32[]{:S(2)}, u32[]{:S(2)}) async-start(bf16[16,112,128]{2,1,0:T(8,128)(2,1)} %pack.2), calls=%async_computation | async-start | bytes 917504 | tf_op jit(solution)/shard_map/all_to_all | solution.py:580
  11.9 23.8 %copy-start.2 = (f32[3,4,4,1024]{3,2,1,0:T(4,128)S(1)}, f32[3,4,4,1024]{3,2,1,0:T(4,128)}, u32[]{:S(2)}) copy-start(f32[3,4,4,1024]{3,2,1,0:T(4,128)} %refs_2_.3) | copy-start | bytes 589828
  11.9 23.8 %copy-start.3 = (f32[3,4,4,1024]{3,2,1,0:T(4,128)S(1)}, f32[3,4,4,1024]{3,2,1,0:T(4,128)}, u32[]{:S(2)}) copy-start(f32[3,4,4,1024]{3,2,1,0:T(4,128)} %refs_3_.3) | copy-start | bytes 589828
  11.9 23.8 %copy-start.4 = (f32[4,4,1024]{2,1,0:T(4,128)S(1)}, f32[4,4,1024]{2,1,0:T(4,128)}, u32[]{:S(2)}) copy-start(f32[4,4,1024]{2,1,0:T(4,128)} %refs_4_.3) | copy-start | bytes 196612
  12.0 23.8 %copy-start.5 = (s32[4,4,1024]{2,1,0:T(4,128)S(1)}, s32[4,4,1024]{2,1,0:T(4,128)}, u32[]{:S(2)}) copy-start(s32[4,4,1024]{2,1,0:T(4,128)} %refs_5_.3) | copy-start | bytes 196612
  12.0 23.8 %copy-start.6 = (s32[4,4]{1,0:T(4,128)S(1)}, s32[4,4]{1,0:T(4,128)}, u32[]{:S(2)}) copy-start(s32[4,4]{1,0:T(4,128)} %refs_0_.3) | copy-start | bytes 196
  27.2 8.2 %collective-permute-start.1 = (bf16[160,128]{1,0:T(8,128)(2,1)S(1)}, bf16[160,128]{1,0:T(8,128)(2,1)S(1)}, u32[]{:S(2)}, u32[]{:S(2)}) collective-permute-start(bf16[160,128]{1,0:T(8,128)(2,1)S(1)} %get-tuple-element.30), channel_id=1, source_target_pairs={{0,16},{16,0},{32,48},{48,32},{64,80},{80,64},{96,112},{112,96},{1... | collective-permute-start | bytes 122888 | tf_op jit(solution)/shard_map/ppermute | solution.py:537
  27.3 8.4 %collective-permute-start = (bf16[160,128]{1,0:T(8,128)(2,1)S(1)}, bf16[160,128]{1,0:T(8,128)(2,1)S(1)}, u32[]{:S(2)}, u32[]{:S(2)}) collective-permute-start(bf16[160,128]{1,0:T(8,128)(2,1)S(1)} %get-tuple-element.31), channel_id=1, source_target_pairs={{0,240},{16,32},{32,16},{48,64},{64,48},{80,96},{96,80},{112,128},... | collective-permute-start | bytes 122888 | tf_op jit(solution)/shard_map/ppermute | solution.py:536
  31.8 19.2 %all-to-all-start.2 = ((bf16[16,112,128]{2,1,0:T(8,128)(2,1)}), bf16[16,112,128]{2,1,0:T(8,128)(2,1)S(1)}, u32[]{:S(2)}, u32[]{:S(2)}) async-start(bf16[16,112,128]{2,1,0:T(8,128)(2,1)} %pack.3), calls=%async_computation.2 | async-start | bytes 917504 | tf_op jit(solution)/shard_map/all_to_all | solution.py:582
  51.0 19.9 %all-to-all-start.1 = ((bf16[16,128,128]{2,1,0:T(8,128)(2,1)}), bf16[16,128,128]{2,1,0:T(8,128)(2,1)S(1)}, u32[]{:S(2)}, u32[]{:S(2)}) async-start(bf16[16,128,128]{2,1,0:T(8,128)(2,1)} %get-tuple-element.18), calls=%async_computation.1 | async-start | bytes 1048576 | tf_op jit(solution)/shard_map/all_to_all | solution.py:605
  64.1 26.5 %copy-start = (f32[3,32,2,2048]{3,2,1,0:T(2,128)S(1)}, f32[3,32,2,2048]{3,2,1,0:T(2,128)}, u32[]{:S(2)}) copy-start(f32[3,32,2,2048]{3,2,1,0:T(2,128)} %param.7) | copy-start | bytes 4718596
  70.9 19.2 %all-to-all-start.3 = ((bf16[16,112,128]{2,1,0:T(8,128)(2,1)}), bf16[16,112,128]{2,1,0:T(8,128)(2,1)S(1)}, u32[]{:S(2)}, u32[]{:S(2)}) async-start(bf16[16,112,128]{2,1,0:T(8,128)(2,1)} %get-tuple-element.24), calls=%async_computation.3 | async-start | bytes 917504 | tf_op jit(solution)/shard_map/all_to_all | solution.py:610
  75.0 3.2 %collective-permute-start.3 = (bf16[6,2048]{1,0:T(8,128)(2,1)S(1)}, bf16[6,2048]{1,0:T(8,128)(2,1)S(1)}, u32[]{:S(2)}, u32[]{:S(2)}) collective-permute-start(bf16[6,2048]{1,0:T(8,128)(2,1)S(1)} %get-tuple-element.34), channel_id=1, source_target_pairs={{0,16},{16,0},{32,48},{48,32},{64,80},{80,64},{96,112},{112,96},{1... | collective-permute-start | bytes 73736 | tf_op jit(solution)/shard_map/ppermute | solution.py:537
  75.1 9.4 %collective-permute-start.2 = (bf16[6,2048]{1,0:T(8,128)(2,1)S(1)}, bf16[6,2048]{1,0:T(8,128)(2,1)S(1)}, u32[]{:S(2)}, u32[]{:S(2)}) collective-permute-start(bf16[6,2048]{1,0:T(8,128)(2,1)S(1)} %get-tuple-element.35), channel_id=1, source_target_pairs={{0,240},{16,32},{32,16},{48,64},{64,48},{80,96},{96,80},{112,128},... | collective-permute-start | bytes 73736 | tf_op jit(solution)/shard_map/ppermute | solution.py:536
  90.6 1.4 %copy-start.1 = (bf16[2,2,3,256,256]{4,3,2,1,0:T(8,128)(2,1)S(1)}, bf16[2,2,3,256,256]{4,3,2,1,0:T(8,128)(2,1)}, u32[]{:S(2)}) copy-start(bf16[2,2,3,256,256]{4,3,2,1,0:T(8,128)(2,1)} %constant.23.clone.taps_ref) | copy-start | bytes 4718596
